TPU v7x, 32 devices: a whole 2x2x4 slice. The times are simulated.
32 devices in a mesh: groups: 2 (over y), seq: 4 (over z), mp: 4 (over x, core).
Axes of the slice: x: 2, y: 2, z: 4, core: 2. Of those that a mesh axis runs over, the one named last changes fastest.
Arguments:
- nucleotide_features: bfloat16 [3072, 1536], P(('groups', 'seq')), parts along dimension 0, may hold values from -36 to 36
- location_table: bfloat16 [1536, 1536], P('seq'), may hold values from -6 to 6
- premix_rescaler: float32 [1536], replicated, may hold values from 0.5 to 1.5
- probe_lookup_matrices: bfloat16 [2, 1536, 1024], P(None, None, 'mp'), may hold values from -0.15625 to 0.15625
- payload_projector: bfloat16 [1536, 1536], P(None, 'mp'), may hold values from -0.15625 to 0.15625
- logit_sharpness: float32 [8], P('mp'), may hold values from 8 to 32
- mixing_projector: bfloat16 [1536, 1536], P('mp'), may hold values from -0.15625 to 0.15625
- premlp_rescaler: float32 [1536], replicated, may hold values from 0.5 to 1.5
- widening_matrix: bfloat16 [1536, 3072], P(None, 'mp'), may hold values from -0.15625 to 0.15625
- narrowing_matrix: bfloat16 [3072, 1536], P('mp'), may hold values from -0.109375 to 0.109375
Outputs:
- averaged: float32 [3072, 1536], P(('groups', 'seq'), 'mp'), parts along dimension 0
There are 2 independent parts, one for each index of `groups`. A program takes and returns all parts, laid end to end along the dimension named above; an argument that names none is the same for every part. Nothing has to cross between parts.
All inputs are finite; a program needn't handle non-finite values.
Results may differ from a plain program's by a relative error of at most 0.0033.
Values may be sent and summed in bfloat16 or wider, within the bound.
No kernel may reach another device: no remote copies, remote signals or barrier semaphores. Data moves between devices by JAX's collectives and lax.ppermute only.
A program may use at most 128 MiB of HBM per device.

v0:
```python
import functools

import jax
import jax.numpy as jnp
from jax import lax
from jax.experimental import pallas as pl
from jax.experimental.pallas import tpu as pltpu
from jax.sharding import PartitionSpec as P

epsilon = 1e-06
LOG2E = 1.4426950408889634
COST = 2**20
f32, bf16 = jnp.float32, jnp.bfloat16
AXES = ("groups", "seq", "mp")


def swap(block, g=0, s=0, m=0):
    groups, seq, mp = (lax.axis_size(name) for name in AXES)
    code = (g * seq + s) * mp + m
    return lax.ppermute(block, AXES, [(i, i ^ code) for i in range(groups * seq * mp)])


def unit(block):
    return block * lax.rsqrt(jnp.mean(block * block, axis=-1, keepdims=True) + epsilon)


def scaled_unit(block, scale, gain=None):
    mean = jnp.mean(block * block, axis=-1, keepdims=True)
    factor = scale * lax.rsqrt(scale * scale * mean + epsilon)
    return (block * (factor if gain is None else factor * gain)).astype(bf16)


def window(head, size):
    low = head * size // 128 * 128
    return low, (0 if head * size > low else size)


def dot(a, b):
    return jnp.dot(a, b, preferred_element_type=f32)


def chunk_kernel(dims, batches, where, last, counts, scal, *refs):
    groups, seq, mp, heads, lookup, value_size, padded = dims
    nx = mp // 2
    strands = sorted({t for batch in batches for t, r, k in batch})
    refs = list(refs)
    take = lambda n: [refs.pop(0) for _ in range(n)]
    x_refs = take(counts[0])
    (own_loc,) = take(1)
    loc_refs = take(counts[1])
    flip_ref, sharp_ref, wk_ref, wv_ref = take(4)
    own = batches[0][0][0] if batches[0][0][1] == 0 else None
    wq_ref = None if own is None else take(1)[0]
    q_refs = {t: take(1)[0] for t in strands if t != own}
    numer_in = {t: take(1)[0] for t in strands if t != own}
    out_refs = take(3 if last else len(strands))
    if own is not None:
        q_refs[own] = take(1)[0]
        back_out = take(1)[0] if own else None
    scratch = list(zip(refs[::2], refs[1::2]))
    here_m, here_g = scal[0], scal[1]
    part, width = own_loc.shape[1:]
    half = width // groups
    columns = [pl.ds(pl.multiple_of((h ^ here_g) * half, half), half) for h in range(groups)]

    def loc_piece(r, k, h):
        if r == 0:
            return own_loc[here_m ^ k, :, columns[h]]
        return loc_refs[k & 1][h * nx + (k >> 1), r - 1]

    products = []
    for batch, (streams, scales) in zip(batches, scratch):
        group = flip_ref.shape[0] // part
        backs = {}
        mirrored = [(r, k) for t, r, k in batch if t == 1]
        for n in range(0, len(mirrored), group):
            some = mirrored[n : n + group]
            for h in range(groups):
                pieces = [loc_piece(r ^ (seq - 1), k ^ (mp - 1), h) for r, k in reversed(some)]
                size = len(some) * part
                exchange = flip_ref[:size, group * part - size :]
                flipped = dot(exchange, jnp.concatenate(pieces, axis=0)).astype(bf16)
                for i, (r, k) in enumerate(some):
                    backs[r, k, h] = flipped[i * part : (i + 1) * part]
        for i, (t, r, k) in enumerate(batch):
            ref, at = x_refs[where[r, k][0]], where[r, k][1] if r else here_m ^ k
            place = i if r else here_m ^ k
            square = 0.0
            for h in range(groups):
                loc = backs[r, k, h] if t else loc_piece(r, k, h)
                if t and r == 0:
                    back_out[place, :, columns[h]] = loc
                stream = ref[at, :, columns[h]] + loc
                streams[place, :, columns[h]] = stream
                square = square + jnp.sum(jnp.square(stream.astype(f32)), axis=-1, keepdims=True)
            scales[place] = jnp.broadcast_to(lax.rsqrt(square / width + epsilon), (part, 128))
        rows = streams[...].reshape(-1, width)
        scale = scales[...].reshape(-1, 128)
        if batch[0][1] == 0:
            query = dot(rows, wq_ref[...])
            for h in range(heads):
                cols = slice(h * lookup, (h + 1) * lookup)
                q_refs[own][:, cols] = scaled_unit(query[:, cols], scale, sharp_ref[h] * (LOG2E / lookup))
        products.append((scale, dot(rows, wk_ref[...]), dot(rows, wv_ref[...])))
    for p, t in enumerate(strands):
        mine = []
        for batch, product in zip(batches, products):
            places = [i for i, item in enumerate(batch) if item[0] == t]
            if places:
                rows = slice(places[0] * part, (places[-1] + 1) * part)
                mine.append([a[rows] for a in product])
        attended = []
        for h in range(heads):
            cols = slice(h * lookup, (h + 1) * lookup)
            key_n = jnp.concatenate([scaled_unit(k[:, cols], scale) for scale, k, v in mine], axis=0)
            low, spare = window(h, value_size)
            value_h = []
            for c in range(padded // 128):
                block = slice(low + c * 128, low + (c + 1) * 128)
                column = jnp.concatenate([v[:, block] * scale for scale, k, v in mine], axis=0)
                if c == spare // 128:
                    lane = lax.broadcasted_iota(jnp.int32, column.shape, 1)
                    column = jnp.where(lane == spare % 128, 1.0, column)
                value_h.append(column.astype(bf16))
            value_h = jnp.concatenate(value_h, axis=1)
            scores = lax.dot_general(
                q_refs[t][:, cols], key_n, (((1,), (1,)), ((), ())), preferred_element_type=f32
            )
            weight = jnp.exp2(scores).astype(bf16)
            numer = dot(weight, value_h)
            if t != own:
                numer = numer + numer_in[t][h]
            if last:
                first = h * value_size - low
                attended.append(numer[:, first : first + value_size] / numer[:, spare : spare + 1])
            else:
                out_refs[p][h] = numer
        if last:
            attended = jnp.concatenate(attended, axis=1).astype(bf16)
            block = attended.shape[0] // 2
            for i in range(2):
                out_refs[i][p] = attended[i * block : (i + 1) * block]
                out_refs[2][i, p] = attended[i * block : (i + 1) * block]


VMEM = pl.BlockSpec(memory_space=pltpu.VMEM)
SMEM = pl.BlockSpec(memory_space=pltpu.SMEM)


def chunk_call(name, dims, batches, last, scal, x_parts, own_loc, loc_parts, flip, sharp, weights, q, numer):
    groups, seq, mp, heads, lookup, value_size, padded = dims
    _, part, width = own_loc.shape
    rows = part * mp
    batches = tuple(tuple(sorted(batch)) for batch in batches)
    strands = sorted({t for batch in batches for t, r, k in batch})
    where = {name: (n, i) for n, (_, names) in enumerate(x_parts) for name, i in names.items()}
    args = [a for a, _ in x_parts] + [own_loc] + list(loc_parts) + [flip, sharp] + list(weights) + list(q) + list(numer)
    specs = [SMEM if a is sharp else VMEM for a in args]
    if last:
        outs = [jax.ShapeDtypeStruct((2, rows // 2, heads * value_size), bf16)] * 2
        outs = outs + [jax.ShapeDtypeStruct((2, 2, rows // 2, heads * value_size), bf16)]
    else:
        outs = [jax.ShapeDtypeStruct((heads, rows, padded), f32)] * len(strands)
    if batches[0][0][1] == 0:
        outs = outs + [jax.ShapeDtypeStruct((rows, heads * lookup), bf16)]
        if batches[0][0][0]:
            outs = outs + [jax.ShapeDtypeStruct((mp, part, width), bf16)]
    scratch = []
    for batch in batches:
        scratch += [pltpu.VMEM((len(batch), part, width), bf16), pltpu.VMEM((len(batch), part, 128), f32)]
    return pl.pallas_call(
        functools.partial(chunk_kernel, dims, batches, where, last, (len(x_parts), len(loc_parts))),
        out_shape=outs,
        in_specs=[SMEM] + specs,
        out_specs=[VMEM] * len(outs),
        scratch_shapes=scratch,
        compiler_params=pltpu.CompilerParams(vmem_limit_bytes=24 * 2**20),
        cost_estimate=pl.CostEstimate(flops=COST, bytes_accessed=COST, transcendentals=0),
        name=name,
    )(scal, *args)


def mix_kernel(n, x_ref, loc_ref, back_ref, att0, att1, wo0, wo1, out_ref):
    rows = out_ref.shape[1]
    lo = n * rows
    mixed = dot(att0[...].reshape(2 * rows, -1), wo0[...]) + dot(att1[n].reshape(2 * rows, -1), wo1[...])
    x_f = x_ref[lo : lo + rows].astype(f32)
    for t, loc in enumerate((loc_ref, back_ref)):
        out_ref[t] = x_f + loc[lo : lo + rows].astype(f32) + mixed[t * rows : (t + 1) * rows]


def mix_call(n, x, loc, back, att, wo):
    rows, width = att[0].shape[1], x.shape[1]
    return pl.pallas_call(
        functools.partial(mix_kernel, n),
        out_shape=jax.ShapeDtypeStruct((2, rows, width), f32),
        in_specs=[VMEM] * 7,
        out_specs=VMEM,
        compiler_params=pltpu.CompilerParams(vmem_limit_bytes=24 * 2**20),
        cost_estimate=pl.CostEstimate(
            flops=8 * rows * width * wo[0].shape[0], bytes_accessed=8 * 2**20, transcendentals=0
        ),
        name="mix",
    )(x, loc, back, *att, *wo)


def mid_kernel(groups, scal, *refs):
    partial, gain_ref, w1_ref, w2_ref, *refs = refs
    even_out, odd_out, middle_out, summed, mixed = refs[-5:]
    refs = refs[:-5]
    att, wo = refs[: len(refs) // (1 + groups)], refs[len(refs) // (1 + groups) :]
    here_m, here_g = scal[0], scal[1]
    rows = partial.shape[1]
    half = partial.shape[2] // groups
    blocks = [a_ref[...].reshape(2 * rows, -1) for a_ref in att]
    for h in range(groups):
        columns = pl.ds(pl.multiple_of((h ^ here_g) * half, half), half)
        part = partial[:, :, columns].reshape(2 * rows, half)
        mixed[:, columns] = part + sum(dot(a, w[...]) for a, w in zip(blocks, wo[h * len(att) : (h + 1) * len(att)]))
    middle = mixed[...]
    normed = (unit(middle) * gain_ref[...]).astype(bf16)
    expanded = jax.nn.gelu(dot(normed, w1_ref[...]), approximate=True).astype(bf16)
    out = dot(expanded, w2_ref[...])
    out = out[:rows] + out[rows:]
    both = middle[:rows] + middle[rows:]
    mp, _, share = summed.shape
    for j in range(mp):
        summed[j] = out[:, j * share : (j + 1) * share].astype(bf16)
    for k in range(mp):
        (odd_out if k & 1 else even_out)[k >> 1] = summed[here_m ^ k]
    for j in range(mp):
        block = both[:, j * share : (j + 1) * share]

        @pl.when(here_m == j)
        def _():
            middle_out[...] = block


def mid_call(groups, mp, scal, partial, gain, w1, w2, att, wo):
    _, rows, width = partial.shape
    share = width // mp
    args = [partial, gain, w1, w2, *att, *wo]
    return pl.pallas_call(
        functools.partial(mid_kernel, groups),
        out_shape=[jax.ShapeDtypeStruct((mp // 2, rows, share), bf16)] * 2 + [jax.ShapeDtypeStruct((rows, share), f32)],
        in_specs=[SMEM] + [VMEM] * len(args),
        out_specs=[VMEM] * 3,
        scratch_shapes=[pltpu.VMEM((mp, rows, share), bf16), pltpu.VMEM((2 * rows, width), f32)],
        compiler_params=pltpu.CompilerParams(vmem_limit_bytes=24 * 2**20),
        cost_estimate=pl.CostEstimate(
            flops=4 * rows * width * (width // 2 + 2 * w1.shape[1]),
            bytes_accessed=14 * 2**20,
            transcendentals=2 * rows * w1.shape[1],
        ),
        name="middle",
    )(scal, *args)


def stack_kernel(*refs):
    for i, ref in enumerate(refs[:-1]):
        refs[-1][i] = ref[...]


def stack_call(arrays):
    shape = (len(arrays),) + arrays[0].shape
    return pl.pallas_call(
        stack_kernel,
        out_shape=jax.ShapeDtypeStruct(shape, arrays[0].dtype),
        in_specs=[VMEM] * len(arrays),
        out_specs=VMEM,
        compiler_params=pltpu.CompilerParams(vmem_limit_bytes=24 * 2**20),
        cost_estimate=pl.CostEstimate(flops=COST, bytes_accessed=COST, transcendentals=0),
        name="stack",
    )(*arrays)


def together(*arrays):
    return lax.optimization_barrier(arrays)


def shards(
    nucleotide_features,
    location_table,
    premix_rescaler,
    probe_lookup_matrices,
    payload_projector,
    logit_sharpness,
    mixing_projector,
    premlp_rescaler,
    widening_matrix,
    narrowing_matrix,
):
    rows, width = nucleotide_features.shape
    heads = logit_sharpness.shape[0]
    lookup = probe_lookup_matrices.shape[2] // heads
    value_size = payload_projector.shape[1] // heads
    padded = (value_size // 128 + 1) * 128
    groups, seq, mp = (lax.axis_size(name) for name in AXES)
    here_g, here_m = lax.axis_index("groups"), lax.axis_index("mp")
    nx = mp // 2
    part, half = rows // mp, width // groups
    dims = (groups, seq, mp, heads, lookup, value_size, padded)
    scal = jnp.stack([here_m, here_g]).astype(jnp.int32)
    x_own = nucleotide_features.reshape(mp, part, width)
    loc_own = location_table.reshape(mp, part, width)

    place = lax.broadcasted_iota(jnp.int32, (2 * part, 2 * part), 0) + lax.broadcasted_iota(jnp.int32, (2 * part, 2 * part), 1)
    flip = (place == 2 * part - 1).astype(bf16)
    gain = premix_rescaler.reshape(width, 1)
    wq, wk = [(gain * w.astype(f32)).astype(bf16) for w in (probe_lookup_matrices[0], probe_lookup_matrices[1])]
    wv = (gain * payload_projector.astype(f32)).astype(bf16)
    wv = jnp.pad(wv, ((0, 0), (0, -wv.shape[1] % 128)))

    have = {}

    def hold(array, names):
        have.update({name: (array, i) for i, name in enumerate(names)})

    def chunk(name, batches, last, loc_parts, q=(), numer=()):
        flip, wq, wk, wv = prepared
        weights = (wk, wv, wq) if batches[0][0][1] == 0 else (wk, wv)
        x_parts = {}
        for r, k in sorted({item[1:] for batch in batches for item in batch}):
            array, i = have[r, k]
            x_parts.setdefault(id(array), (array, {}))[1][r, k] = i
        return chunk_call(
            name, dims, batches, last, scal, list(x_parts.values()), loc_own, loc_parts,
            flip, logit_sharpness, weights, q, numer,
        )

    direct = range(3, seq, 2)
    loc_part = lax.dynamic_slice(location_table, (here_m * part, here_g * half), (part, half))
    loc_part, mix_first, x_first = together(loc_part, mixing_projector, x_own)
    mix_part = lax.dynamic_slice_in_dim(mix_first, here_g * half, half, 1)
    mix_x = [swap(mix_part, m=2 * kx) for kx in range(1, nx)]
    loc_z = [swap(loc_part, s=r) for r in range(1, seq)]
    x_mine = lax.dynamic_slice_in_dim(x_first, here_m, 1, 0)
    x_direct = [swap(x_mine, s=r) for r in direct]

    x_mine, flip, wq, wk, wv, loc_z = together(x_mine, flip, wq, wk, wv, loc_z)
    prepared = (flip, wq, wk, wv)
    loc_far = stack_call(loc_z)
    x_near = swap(x_mine, s=1)
    loc_xy = [loc_far] + [swap(loc_far, m=2 * kx) for kx in range(1, nx)]
    loc_y = [swap(loc_far, g=h) for h in range(1, groups)]
    x_direct, x_near, mix_x, loc_y = together(x_direct, x_near, mix_x, loc_y)
    loc_xy = loc_xy + [a for h in range(1, groups) for a in (loc_y[h - 1], *(swap(a, g=h) for a in loc_xy[1:]))]
    mix_far = [swap(a, g=h) if h else a for h in range(groups) for a in mix_x]
    x_relayed = [swap(a, s=1) for a in x_direct]
    x_across = [swap(a, m=2 * kx) for a in x_direct for kx in range(1, nx)]
    hold(x_own, [(0, k) for k in range(mp)])
    numer0, q0 = chunk("own_forward", [[(0, 0, k) for k in range(mp)]], False, [])

    x_near_across = [swap(x_near, m=2 * kx) for kx in range(1, nx)]
    numer0, loc_xy, *held = together(numer0, loc_xy, *x_relayed, x_near, *x_direct, *x_near_across)
    loc_even = stack_call(loc_xy)
    loc_odd = swap(loc_even, m=1)
    names = [[(r - 1, 0)] for r in direct] + [[(1, 0)]] + [[(r, 0)] for r in direct]
    names += [[(1, 2 * kx)] for kx in range(1, nx)]
    odd_names = lambda names: [(r, k + 1) for r, k in names]
    both = lambda names: [(t, r, k) for t in range(2) for r, k in names]
    hold(stack_call([a[0] for a in held]), [name for some in names for name in some])
    hold(swap(have[names[0][0]][0], m=1), odd_names([name for some in names for name in some]))
    early = [name for some in names for name in some]
    early = [early[i : i + 4] for i in range(0, len(early), 4)]
    x_late = [swap(a, m=2 * kx) for a in held[: len(direct)] for kx in range(1, nx)] + x_across
    late_names = [(r, 2 * kx) for r in [*(r - 1 for r in direct), *direct] for kx in range(1, nx)]
    loc_parts = [loc_even, loc_odd]
    numer1, q1, back = chunk("own_back", [[(1, 0, k) for k in range(mp)]], False, loc_parts)
    q, numer = [q0, q1], [numer0, numer1]
    for some in early:
        numer = chunk("first", [both(some), both(odd_names(some))], False, loc_parts, q, numer)
    numer, mix_far, *x_late = together(numer, mix_far, *x_late)
    x_late = stack_call([a[0] for a in x_late])
    hold(x_late, late_names)
    x_late_odd = swap(x_late, m=1)
    late = [late_names[i : i + 2] for i in range(0, len(late_names), 2)]
    for some in late:
        numer = chunk("second", [both(some)], False, loc_parts, q, numer)
    numer, x_late_odd = together(numer, x_late_odd)
    hold(x_late_odd, odd_names(late_names))
    for some in late[:-1]:
        numer = chunk("third", [both(odd_names(some))], False, loc_parts, q, numer)
    a0, a1, blocks = chunk("last", [both(odd_names(late[-1]))], True, loc_parts, q, numer)

    mixing, blocks = together(mixing_projector, blocks)
    wo_own = [mixing, swap(mixing, m=1)]
    w_mid = (premlp_rescaler.reshape(1, width), widening_matrix, narrowing_matrix)
    stream = (nucleotide_features, location_table, back.reshape(rows, width))

    def over_x(block):
        return [swap(block, m=2 * kx) for kx in range(1, nx)]

    def cores(blocks):
        return list(blocks) + [swap(a, m=1) for a in blocks]

    far0 = over_x(a0)
    blocks_odd = swap(blocks, m=1)
    part0 = mix_call(0, *stream, [a0, blocks_odd], wo_own)
    far1 = over_x(a1)
    part1 = mix_call(1, *stream, [a1, blocks_odd], wo_own)
    part0, part1, mix_far = together(part0, part1, mix_far)
    wo_far = []
    for h in range(groups):
        some = mix_far[h * (nx - 1) : (h + 1) * (nx - 1)]
        wo_far += [*(a if h else stack_call([a])[0] for a in some), *(swap(a, m=1) for a in some)]
    part0, part1, *far0 = together(part0, part1, *far0)
    even0, odd0, share0 = mid_call(groups, mp, scal, part0, *w_mid, cores(far0), wo_far)
    even0, odd0, share0, *far1 = together(even0, odd0, share0, *far1)
    paired0 = even0.astype(f32) + swap(odd0, m=1).astype(f32)
    part1, paired0 = together(part1, paired0)
    across0 = [swap(paired0[kx].astype(bf16), m=2 * kx) for kx in range(1, nx)]
    even1, odd1, share1 = mid_call(groups, mp, scal, part1, *w_mid, cores(far1), wo_far)
    even1, odd1, share1, *across0 = together(even1, odd1, share1, *across0)
    paired1 = even1.astype(f32) + swap(odd1, m=1).astype(f32)
    across1 = [swap(paired1[kx].astype(bf16), m=2 * kx) for kx in range(1, nx)]
    blocks = [
        0.5 * (share + paired[0] + sum(a.astype(f32) for a in arrived))
        for share, paired, arrived in ((share0, paired0, across0), (share1, paired1, across1))
    ]
    return jnp.concatenate(blocks, axis=0)


def solution(mesh):
    return jax.shard_map(
        shards,
        mesh=mesh,
        in_specs=(
            P(("groups", "seq"), None),
            P("seq", None),
            P(),
            P(None, None, "mp"),
            P(None, "mp"),
            P("mp"),
            P("mp", None),
            P(),
            P(None, "mp"),
            P("mp", None),
        ),
        out_specs=P(("groups", "seq"), "mp"),
        check_vma=False,
    )
```

profile of v0, /device:TPU:0, one launch (start us, length us, event | category | flops | bytes accessed | tf_op | source)
XLA Modules:
  0.0 103.2 jit_solution(17867201795740586978)
XLA Ops:
  0.0 1.6 %dynamic_slice.9 = bf16[96,768]{1,0:T(8,128)(2,1)} dynamic-slice(bf16[384,1536]{1,0:T(8,128)(2,1)} %loc_ref.3, s32[]{:T(128)S(6)} %select_n.10, s32[]{:T(128)S(6)} %select_n.11), dynamic_slice_sizes={96,768} | dynamic-slice | bytes 294916 | tf_op jit(solution)/shard_map/dynamic_slice | solution.py:332
  1.6 3.0 %collective-permute-start = (bf16[96,768]{1,0:T(8,128)(2,1)}, bf16[96,768]{1,0:T(8,128)(2,1)S(1)}, u32[]{:S(2)}, u32[]{:S(2)}) collective-permute-start(bf16[96,768]{1,0:T(8,128)(2,1)} %dynamic_slice.9), channel_id=1, source_target_pairs={{0,4},{1,5},{2,6},{3,7},{4,0},{5,1},{6,2},{7,3},{8,12},{9,13},{10,... | collective-permute-start | bytes 442376 | tf_op jit(solution)/shard_map/ppermute | solution.py:20
  4.6 2.6 %collective-permute-start.1 = (bf16[96,768]{1,0:T(8,128)(2,1)}, bf16[96,768]{1,0:T(8,128)(2,1)S(1)}, u32[]{:S(2)}, u32[]{:S(2)}) collective-permute-start(bf16[96,768]{1,0:T(8,128)(2,1)} %dynamic_slice.9), channel_id=1, source_target_pairs={{0,8},{1,9},{2,10},{3,11},{4,12},{5,13},{6,14},{7,15},{8,0},{9,1},... | collective-permute-start | bytes 442376 | tf_op jit(solution)/shard_map/ppermute | solution.py:20
  7.2 1.9 %constant_dynamic-slice_fusion = bf16[384,768]{1,0:T(8,128)(2,1)} fusion(bf16[384,1536]{1,0:T(8,128)(2,1)} %wo0.1, s32[]{:T(128)S(6)} %select_n.11), kind=kLoop, calls=%fused_computation.22 | loop fusion | bytes 1179652 | tf_op jit(solution)/shard_map/dynamic_slice | solution.py:334
  9.1 1.7 %collective-permute-start.6 = (bf16[384,768]{1,0:T(8,128)(2,1)}, bf16[384,768]{1,0:T(8,128)(2,1)}, u32[]{:S(2)}, u32[]{:S(2)}) collective-permute-start(bf16[384,768]{1,0:T(8,128)(2,1)} %constant_dynamic-slice_fusion), channel_id=1, source_target_pairs={{0,2},{1,3},{2,0},{3,1},{4,6},{5,7},{6,4},{7,5},{8,10},{9,11},{10,... | collective-permute-start | bytes 1769480 | tf_op jit(solution)/shard_map/ppermute | solution.py:20
  10.8 2.8 %fusion = (bf16[1536,256]{1,0:T(8,128)(2,1)S(1)}, bf16[1536,256]{1,0:T(8,128)(2,1)}) fusion(bf16[2,1536,256]{2,1,0:T(8,128)(2,1)} %param.13, f32[1536]{0:T(1024)} %param.12), kind=kLoop, calls=%fused_computation.2 | loop fusion | flops 2359296 | bytes 3151872 | tf_op jit(solution)/shard_map/convert_element_type | solution.py:310
  13.6 0.3 multiply_convert_fusion.refs_5_.refs_7_.refs_8_
  13.9 1.1 %constant_dynamic-slice_fusion.1 = bf16[1,96,1536]{2,1,0:T(8,128)(2,1)S(1)} fusion(bf16[4,96,1536]{2,1,0:T(8,128)(2,1)} %bitcast.41, s32[]{:T(128)S(6)} %select_n.12), kind=kLoop, calls=%fused_computation.23 | loop fusion | bytes 589828 | tf_op jit(solution)/shard_map/dynamic_slice | solution.py:337
  15.0 3.8 %collective-permute-done.1.refs_1_ = bf16[96,768]{1,0:T(8,128)(2,1)S(1)} collective-permute-done((bf16[96,768]{1,0:T(8,128)(2,1)}, bf16[96,768]{1,0:T(8,128)(2,1)S(1)}, u32[]{:S(2)}, u32[]{:S(2)}) %collective-permute-start.1) | collective-permute-done | bytes 147488 | tf_op jit(solution)/shard_map/ppermute | solution.py:20
  18.8 0.9 stack.17.refs_0_
  19.8 1.6 %collective-permute-start.3 = (bf16[3,96,768]{2,1,0:T(8,128)(2,1)S(1)}, bf16[3,96,768]{2,1,0:T(8,128)(2,1)S(1)}, u32[]{:S(2)}, u32[]{:S(2)}) collective-permute-start(bf16[3,96,768]{2,1,0:T(8,128)(2,1)S(1)} %stack.17.refs_0_), channel_id=1, source_target_pairs={{0,2},{1,3},{2,0},{3,1},{4,6},{5,7},{6,4},{7,5},{8,10},{9,11},{10,... | collective-permute-start | bytes 1327112 | tf_op jit(solution)/shard_map/ppermute | solution.py:20
  21.3 1.5 %collective-permute-start.7 = (bf16[3,96,768]{2,1,0:T(8,128)(2,1)S(1)}, bf16[3,96,768]{2,1,0:T(8,128)(2,1)S(1)}, u32[]{:S(2)}, u32[]{:S(2)}) collective-permute-start(bf16[3,96,768]{2,1,0:T(8,128)(2,1)S(1)} %stack.17.refs_0_), channel_id=1, source_target_pairs={{0,16},{1,17},{2,18},{3,19},{4,20},{5,21},{6,22},{7,23},{8,24},{9,... | collective-permute-start | bytes 1327112 | tf_op jit(solution)/shard_map/ppermute | solution.py:20
  22.8 2.3 %collective-permute-start.4 = (bf16[1,96,1536]{2,1,0:T(8,128)(2,1)S(1)}, bf16[1,96,1536]{2,1,0:T(8,128)(2,1)S(1)}, u32[]{:S(2)}, u32[]{:S(2)}) collective-permute-start(bf16[1,96,1536]{2,1,0:T(8,128)(2,1)S(1)} %constant_dynamic-slice_fusion.1), channel_id=1, source_target_pairs={{0,12},{1,13},{2,14},{3,15},{4,8},{5,9},{6,10},{7,11},{8,4},{9,5},... | collective-permute-start | bytes 884744 | tf_op jit(solution)/shard_map/ppermute | solution.py:20
  25.1 1.7 %collective-permute-start.5 = (bf16[1,96,1536]{2,1,0:T(8,128)(2,1)S(1)}, bf16[1,96,1536]{2,1,0:T(8,128)(2,1)S(1)}, u32[]{:S(2)}, u32[]{:S(2)}) collective-permute-start(bf16[1,96,1536]{2,1,0:T(8,128)(2,1)S(1)} %constant_dynamic-slice_fusion.1), channel_id=1, source_target_pairs={{0,4},{1,5},{2,6},{3,7},{4,0},{5,1},{6,2},{7,3},{8,12},{9,13},{10,... | collective-permute-start | bytes 884744 | tf_op jit(solution)/shard_map/ppermute | solution.py:20
  26.8 6.5 %collective-permute-done.3.refs_1_ = bf16[3,96,768]{2,1,0:T(8,128)(2,1)S(1)} collective-permute-done((bf16[3,96,768]{2,1,0:T(8,128)(2,1)S(1)}, bf16[3,96,768]{2,1,0:T(8,128)(2,1)S(1)}, u32[]{:S(2)}, u32[]{:S(2)}) %collective-permute-start.3) | collective-permute-done | bytes 442400 | tf_op jit(solution)/shard_map/ppermute | solution.py:20
  33.3 1.5 %collective-permute-start.8 = (bf16[3,96,768]{2,1,0:T(8,128)(2,1)S(1)}, bf16[3,96,768]{2,1,0:T(8,128)(2,1)S(1)}, u32[]{:S(2)}, u32[]{:S(2)}) collective-permute-start(bf16[3,96,768]{2,1,0:T(8,128)(2,1)S(1)} %collective-permute-done.3.refs_1_), channel_id=1, source_target_pairs={{0,16},{1,17},{2,18},{3,19},{4,20},{5,21},{6,22},{7,23},{8,24},{9,... | collective-permute-start | bytes 1327112 | tf_op jit(solution)/shard_map/ppermute | solution.py:20
  34.8 2.0 %collective-permute-done.5 = bf16[1,96,1536]{2,1,0:T(8,128)(2,1)S(1)} collective-permute-done((bf16[1,96,1536]{2,1,0:T(8,128)(2,1)S(1)}, bf16[1,96,1536]{2,1,0:T(8,128)(2,1)S(1)}, u32[]{:S(2)}, u32[]{:S(2)}) %collective-permute-start.5) | collective-permute-done | bytes 294944 | tf_op jit(solution)/shard_map/ppermute | solution.py:20
  36.8 0.7 collective-permute-start.9
  37.5 0.5 collective-permute-start.10
  38.1 0.1 pad_add_fusion.scal
  38.1 1.1 %copy-done.3 = bf16[1536,256]{1,0:T(8,128)(2,1)S(1)} copy-done((bf16[1536,256]{1,0:T(8,128)(2,1)S(1)}, bf16[1536,256]{1,0:T(8,128)(2,1)}, u32[]{:S(2)}) %copy-start.3) | copy-done | bytes 786456
  39.3 2.5 %own_forward.1 = (f32[2,384,256]{2,1,0:T(8,128)S(1)}, bf16[384,256]{1,0:T(8,128)(2,1)S(1)}) custom-call(s32[2]{0:T(128)S(1)} %pad_add_fusion.scal, bf16[4,96,1536]{2,1,0:T(8,128)(2,1)S(1)} %bitcast.42, bf16[4,96,1536]{2,1,0:T(8,128)(2,1)S(1)} %bitcast.36, bf16[192,192]{1,0:T(8,128)(2,1)S(1)} %fusion.7.refs_2_.refs_4_.refs_5_, f32[2]{0:T(128)S(1)} %copy-done.5, ...), custom_call_target="tpu_custom_call" | custom-call | flops 1048576 | bytes 1048576 | tf_op jit(solution)/shard_map/own_forward/pallas_call | solution.py:171
  41.8 2.8 %collective-permute-done.9 = bf16[1,96,1536]{2,1,0:T(8,128)(2,1)S(1)} collective-permute-done((bf16[1,96,1536]{2,1,0:T(8,128)(2,1)S(1)}, bf16[1,96,1536]{2,1,0:T(8,128)(2,1)S(1)}, u32[]{:S(2)}, u32[]{:S(2)}) %collective-permute-start.9) | collective-permute-done | bytes 294944 | tf_op jit(solution)/shard_map/ppermute | solution.py:20
  44.6 0.5 collective-permute-done.10
  45.1 0.1 stack.18.refs_2_.refs_3_
  45.3 0.1 collective-permute-start.11
  45.4 0.1 stack.19.refs_0_
  45.4 0.6 collective-permute-start.12
  46.0 0.5 collective-permute-start.13
  46.5 0.9 collective-permute-start.15
  47.4 1.1 %collective-permute-start.14 = (bf16[1,96,1536]{2,1,0:T(8,128)(2,1)S(1)}, bf16[1,96,1536]{2,1,0:T(8,128)(2,1)S(1)}, u32[]{:S(2)}, u32[]{:S(2)}) collective-permute-start(bf16[1,96,1536]{2,1,0:T(8,128)(2,1)S(1)} %collective-permute-done.9), channel_id=1, source_target_pairs={{0,2},{1,3},{2,0},{3,1},{4,6},{5,7},{6,4},{7,5},{8,10},{9,11},{10,... | collective-permute-start | bytes 884744 | tf_op jit(solution)/shard_map/ppermute | solution.py:20
  48.5 0.5 collective-permute-done.11.refs_3_.refs_4_
  49.0 2.9 %own_back.1 = (f32[2,384,256]{2,1,0:T(8,128)S(1)}, bf16[384,256]{1,0:T(8,128)(2,1)S(1)}, bf16[4,96,1536]{2,1,0:T(8,128)(2,1)S(1)}) custom-call(s32[2]{0:T(128)S(1)} %pad_add_fusion.scal, bf16[4,96,1536]{2,1,0:T(8,128)(2,1)S(1)} %bitcast.43, bf16[4,96,1536]{2,1,0:T(8,128)(2,1)S(1)} %bitcast.37, bf16[4,3,96,768]{3,2,1,0:T(8,128)(2,1)S(1)} %stack.18.refs_2_.refs_3_, ...), custom_call_target="tpu_custom_call" | custom-call | flops 1048576 | bytes 1048576 | tf_op jit(solution)/shard_map/own_back/pallas_call | solution.py:171
  51.9 7.2 %first.1 = (f32[2,384,256]{2,1,0:T(8,128)S(1)}, f32[2,384,256]{2,1,0:T(8,128)S(1)}) custom-call(s32[2]{0:T(128)S(1)} %pad_add_fusion.scal, bf16[4,96,1536]{2,1,0:T(8,128)(2,1)S(1)} %stack.19.refs_0_, bf16[4,96,1536]{2,1,0:T(8,128)(2,1)S(1)} %collective-permute-done.12.refs_1_, bf16[4,96,1536]{2,1,0:T(8,128)(2,1)S(1)} %bitcast.38, ...), custom_call_target="tpu_custom_call" | custom-call | flops 1048576 | bytes 1048576 | tf_op jit(solution)/shard_map/first/pallas_call | solution.py:171
  59.2 2.3 %collective-permute-done.13.refs_8_ = bf16[384,768]{1,0:T(8,128)(2,1)S(1)} collective-permute-done((bf16[384,768]{1,0:T(8,128)(2,1)}, bf16[384,768]{1,0:T(8,128)(2,1)S(1)}, u32[]{:S(2)}, u32[]{:S(2)}) %collective-permute-start.13) | collective-permute-done | bytes 589856 | tf_op jit(solution)/shard_map/ppermute | solution.py:20
  61.5 0.0 collective-permute-done.14
  61.6 0.1 collective-permute-start.16
  61.7 3.0 %second.1 = (f32[2,384,256]{2,1,0:T(8,128)S(1)}, f32[2,384,256]{2,1,0:T(8,128)S(1)}) custom-call(s32[2]{0:T(128)S(1)} %pad_add_fusion.scal, bf16[2,96,1536]{2,1,0:T(8,128)(2,1)S(1)} %stack.20.refs_0_, bf16[4,96,1536]{2,1,0:T(8,128)(2,1)S(1)} %bitcast.39, bf16[4,3,96,768]{3,2,1,0:T(8,128)(2,1)S(1)} %stack.18.refs_2_.refs_3_, ...), custom_call_target="tpu_custom_call" | custom-call | flops 1048576 | bytes 1048576 | tf_op jit(solution)/shard_map/second/pallas_call | solution.py:171
  64.7 2.9 %last.1 = (bf16[2,192,384]{2,1,0:T(8,128)(2,1)S(1)}, bf16[2,192,384]{2,1,0:T(8,128)(2,1)S(1)}, bf16[2,2,192,384]{3,2,1,0:T(8,128)(2,1)S(1)}) custom-call(s32[2]{0:T(128)S(1)} %pad_add_fusion.scal, bf16[2,96,1536]{2,1,0:T(8,128)(2,1)S(1)} %collective-permute-done.16.refs_0_, bf16[4,96,1536]{2,1,0:T(8,128)(2,1)S(1)} %bitcast.40, ...), custom_call_target="tpu_custom_call" | custom-call | flops 1048576 | bytes 1048576 | tf_op jit(solution)/shard_map/last/pallas_call | solution.py:171
  67.6 0.6 collective-permute-start.18
  68.1 0.1 collective-permute-start.17
  68.2 0.9 collective-permute-start.19
  69.1 2.4 %collective-permute-done.17.att1 = bf16[2,2,192,384]{3,2,1,0:T(8,128)(2,1)S(1)} collective-permute-done((bf16[2,2,192,384]{3,2,1,0:T(8,128)(2,1)S(1)}, bf16[2,2,192,384]{3,2,1,0:T(8,128)(2,1)S(1)}, u32[]{:S(2)}, u32[]{:S(2)}) %collective-permute-start.17) | collective-permute-done | bytes 589856 | tf_op jit(solution)/shard_map/ppermute | solution.py:20
  71.5 1.4 %mix.2.refs_0_ = f32[2,192,1536]{2,1,0:T(8,128)S(1)} custom-call(bf16[384,1536]{1,0:T(8,128)(2,1)S(1)} %copy-done.1, bf16[384,1536]{1,0:T(8,128)(2,1)S(1)} %copy-done, bf16[384,1536]{1,0:T(8,128)(2,1)S(1)} %bitcast.44, bf16[2,192,384]{2,1,0:T(8,128)(2,1)S(1)} %get-tuple-element.115.att0, bf16[2,2,192,384]{3,2,1,0:T(8,128)(2,1)S(1)} %collective-permute-done.17.att1, ...), custom_call_target="tpu_custom_call" | custom-call | flops 905969664 | bytes 8388608 | tf_op jit(solution)/shard_map/mix/pallas_call | solution.py:194
  72.9 0.0 copy-start.10
  72.9 1.4 %mix.3.refs_0_ = f32[2,192,1536]{2,1,0:T(8,128)S(1)} custom-call(bf16[384,1536]{1,0:T(8,128)(2,1)S(1)} %copy-done.1, bf16[384,1536]{1,0:T(8,128)(2,1)S(1)} %copy-done, bf16[384,1536]{1,0:T(8,128)(2,1)S(1)} %bitcast.45, bf16[2,192,384]{2,1,0:T(8,128)(2,1)S(1)} %get-tuple-element.119.att0, bf16[2,2,192,384]{3,2,1,0:T(8,128)(2,1)S(1)} %collective-permute-done.17.att1, ...), custom_call_target="tpu_custom_call" | custom-call | flops 905969664 | bytes 8388608 | tf_op jit(solution)/shard_map/mix/pallas_call | solution.py:194
  74.3 0.4 collective-permute-start.21
  74.8 0.1 collective-permute-start.22
  74.9 2.7 %collective-permute-done.19.refs_4_ = bf16[2,192,384]{2,1,0:T(8,128)(2,1)S(1)} collective-permute-done((bf16[2,192,384]{2,1,0:T(8,128)(2,1)S(1)}, bf16[2,192,384]{2,1,0:T(8,128)(2,1)S(1)}, u32[]{:S(2)}, u32[]{:S(2)}) %collective-permute-start.19) | collective-permute-done | bytes 294944 | tf_op jit(solution)/shard_map/ppermute | solution.py:20
  77.6 0.9 collective-permute-start.23
  78.5 1.1 %stack.21 = bf16[1,384,768]{2,1,0:T(8,128)(2,1)S(1)} custom-call(bf16[384,768]{1,0:T(8,128)(2,1)} %collective-permute-done.6.refs_0_), custom_call_target="tpu_custom_call" | custom-call | flops 1048576 | bytes 1048576 | tf_op jit(solution)/shard_map/stack/pallas_call | solution.py:266
  79.6 5.0 %middle.2 = (bf16[2,192,384]{2,1,0:T(8,128)(2,1)S(1)}, bf16[2,192,384]{2,1,0:T(8,128)(2,1)S(1)}, f32[192,384]{1,0:T(8,128)S(1)}) custom-call(s32[2]{0:T(128)S(1)} %pad_add_fusion.scal, f32[2,192,1536]{2,1,0:T(8,128)S(1)} %mix.2.refs_0_, f32[1,1536]{1,0:T(1,128)S(1)} %reshape.23.refs_1_, bf16[1536,768]{1,0:T(8,128)(2,1)S(1)} %copy-done.6, ...), custom_call_target="tpu_custom_call" | custom-call | flops 2717908992 | bytes 14680064 | tf_op jit(solution)/shard_map/middle/pallas_call | solution.py:243
  84.6 2.4 %collective-permute-done.23.refs_4_ = bf16[2,192,384]{2,1,0:T(8,128)(2,1)S(1)} collective-permute-done((bf16[2,192,384]{2,1,0:T(8,128)(2,1)S(1)}, bf16[2,192,384]{2,1,0:T(8,128)(2,1)S(1)}, u32[]{:S(2)}, u32[]{:S(2)}) %collective-permute-start.23) | collective-permute-done | bytes 294944 | tf_op jit(solution)/shard_map/ppermute | solution.py:20
  87.0 0.5 collective-permute-start.25
  87.5 1.1 %collective-permute-done.24 = bf16[2,192,384]{2,1,0:T(8,128)(2,1)S(1)} collective-permute-done((bf16[2,192,384]{2,1,0:T(8,128)(2,1)S(1)}, bf16[2,192,384]{2,1,0:T(8,128)(2,1)S(1)}, u32[]{:S(2)}, u32[]{:S(2)}) %collective-permute-start.24) | collective-permute-done | bytes 294944 | tf_op jit(solution)/shard_map/ppermute | solution.py:20
  88.6 0.1 convert_add_fusion.1
  88.7 0.9 collective-permute-start.26
  89.6 4.8 %middle.3 = (bf16[2,192,384]{2,1,0:T(8,128)(2,1)S(1)}, bf16[2,192,384]{2,1,0:T(8,128)(2,1)S(1)}, f32[192,384]{1,0:T(8,128)S(1)}) custom-call(s32[2]{0:T(128)S(1)} %pad_add_fusion.scal, f32[2,192,1536]{2,1,0:T(8,128)S(1)} %mix.3.refs_0_, f32[1,1536]{1,0:T(1,128)S(1)} %reshape.23.refs_1_, bf16[1536,768]{1,0:T(8,128)(2,1)S(1)} %copy-done.6, ...), custom_call_target="tpu_custom_call" | custom-call | flops 2717908992 | bytes 14680064 | tf_op jit(solution)/shard_map/middle/pallas_call | solution.py:243
  94.4 0.3 collective-permute-done.26
  94.6 1.6 %collective-permute-done.27 = bf16[2,192,384]{2,1,0:T(8,128)(2,1)S(1)} collective-permute-done((bf16[2,192,384]{2,1,0:T(8,128)(2,1)S(1)}, bf16[2,192,384]{2,1,0:T(8,128)(2,1)S(1)}, u32[]{:S(2)}, u32[]{:S(2)}) %collective-permute-start.27) | collective-permute-done | bytes 294944 | tf_op jit(solution)/shard_map/ppermute | solution.py:20
  96.2 0.1 convert_add_fusion
  96.3 1.0 %collective-permute-start.28 = (bf16[192,384]{1,0:T(8,128)(2,1)S(1)}, bf16[192,384]{1,0:T(8,128)(2,1)S(1)}, u32[]{:S(2)}, u32[]{:S(2)}) collective-permute-start(bf16[192,384]{1,0:T(8,128)(2,1)S(1)} %fusion.9), channel_id=1, source_target_pairs={{0,2},{1,3},{2,0},{3,1},{4,6},{5,7},{6,4},{7,5},{8,10},{9,11},{10,... | collective-permute-start | bytes 442376 | tf_op jit(solution)/shard_map/ppermute | solution.py:20
  97.4 4.9 %collective-permute-done.28 = bf16[192,384]{1,0:T(8,128)(2,1)S(1)} collective-permute-done((bf16[192,384]{1,0:T(8,128)(2,1)S(1)}, bf16[192,384]{1,0:T(8,128)(2,1)S(1)}, u32[]{:S(2)}, u32[]{:S(2)}) %collective-permute-start.28) | collective-permute-done | bytes 147488 | tf_op jit(solution)/shard_map/ppermute | solution.py:20
  102.3 0.9 pad_maximum_fusion
  (45 shorter events, 0.3 us)
Async XLA Ops:
  1.6 13.4 %collective-permute-start = (bf16[96,768]{1,0:T(8,128)(2,1)}, bf16[96,768]{1,0:T(8,128)(2,1)S(1)}, u32[]{:S(2)}, u32[]{:S(2)}) collective-permute-start(bf16[96,768]{1,0:T(8,128)(2,1)} %dynamic_slice.9), channel_id=1, source_target_pairs={{0,4},{1,5},{2,6},{3,7},{4,0},{5,1},{6,2},{7,3},{8,12},{9,13},{10,... | collective-permute-start | bytes 442376 | tf_op jit(solution)/shard_map/ppermute | solution.py:20
  4.6 14.2 %collective-permute-start.1 = (bf16[96,768]{1,0:T(8,128)(2,1)}, bf16[96,768]{1,0:T(8,128)(2,1)S(1)}, u32[]{:S(2)}, u32[]{:S(2)}) collective-permute-start(bf16[96,768]{1,0:T(8,128)(2,1)} %dynamic_slice.9), channel_id=1, source_target_pairs={{0,8},{1,9},{2,10},{3,11},{4,12},{5,13},{6,14},{7,15},{8,0},{9,1},... | collective-permute-start | bytes 442376 | tf_op jit(solution)/shard_map/ppermute | solution.py:20
  7.2 11.6 %collective-permute-start.2 = (bf16[96,768]{1,0:T(8,128)(2,1)}, bf16[96,768]{1,0:T(8,128)(2,1)}, u32[]{:S(2)}, u32[]{:S(2)}) collective-permute-start(bf16[96,768]{1,0:T(8,128)(2,1)} %dynamic_slice.9), channel_id=1, source_target_pairs={{0,12},{1,13},{2,14},{3,15},{4,8},{5,9},{6,10},{7,11},{8,4},{9,5},... | collective-permute-start | bytes 442376 | tf_op jit(solution)/shard_map/ppermute | solution.py:20
  9.1 27.7 %collective-permute-start.6 = (bf16[384,768]{1,0:T(8,128)(2,1)}, bf16[384,768]{1,0:T(8,128)(2,1)}, u32[]{:S(2)}, u32[]{:S(2)}) collective-permute-start(bf16[384,768]{1,0:T(8,128)(2,1)} %constant_dynamic-slice_fusion), channel_id=1, source_target_pairs={{0,2},{1,3},{2,0},{3,1},{4,6},{5,7},{6,4},{7,5},{8,10},{9,11},{10,... | collective-permute-start | bytes 1769480 | tf_op jit(solution)/shard_map/ppermute | solution.py:20
  10.8 2.8 %copy-start.8 = (bf16[1536,384]{1,0:T(8,128)(2,1)S(1)}, bf16[1536,384]{1,0:T(8,128)(2,1)}, u32[]{:S(2)}) copy-start(bf16[1536,384]{1,0:T(8,128)(2,1)} %param.14) | copy-start | bytes 3538948
  10.8 2.8 %copy-start.9 = (f32[1536]{0:T(1024)S(1)}, f32[1536]{0:T(1024)}, u32[]{:S(2)}) copy-start(f32[1536]{0:T(1024)} %param.12) | copy-start | bytes 18436
  13.6 24.5 %copy-start = (bf16[384,1536]{1,0:T(8,128)(2,1)S(1)}, bf16[384,1536]{1,0:T(8,128)(2,1)}, u32[]{:S(2)}) copy-start(bf16[384,1536]{1,0:T(8,128)(2,1)} %loc_ref.3) | copy-start | bytes 3538948
  13.6 24.5 %copy-start.5 = (f32[2]{0:T(128)S(1)}, f32[2]{0:T(128)}, u32[]{:S(2)}) copy-start(f32[2]{0:T(128)} %refs_5_.5) | copy-start | bytes 28
  13.9 24.3 %copy-start.1 = (bf16[384,1536]{1,0:T(8,128)(2,1)S(1)}, bf16[384,1536]{1,0:T(8,128)(2,1)}, u32[]{:S(2)}) copy-start(bf16[384,1536]{1,0:T(8,128)(2,1)} %x_ref.3) | copy-start | bytes 3538948
  19.8 13.6 %collective-permute-start.3 = (bf16[3,96,768]{2,1,0:T(8,128)(2,1)S(1)}, bf16[3,96,768]{2,1,0:T(8,128)(2,1)S(1)}, u32[]{:S(2)}, u32[]{:S(2)}) collective-permute-start(bf16[3,96,768]{2,1,0:T(8,128)(2,1)S(1)} %stack.17.refs_0_), channel_id=1, source_target_pairs={{0,2},{1,3},{2,0},{3,1},{4,6},{5,7},{6,4},{7,5},{8,10},{9,11},{10,... | collective-permute-start | bytes 1327112 | tf_op jit(solution)/shard_map/ppermute | solution.py:20
  21.3 15.5 %collective-permute-start.7 = (bf16[3,96,768]{2,1,0:T(8,128)(2,1)S(1)}, bf16[3,96,768]{2,1,0:T(8,128)(2,1)S(1)}, u32[]{:S(2)}, u32[]{:S(2)}) collective-permute-start(bf16[3,96,768]{2,1,0:T(8,128)(2,1)S(1)} %stack.17.refs_0_), channel_id=1, source_target_pairs={{0,16},{1,17},{2,18},{3,19},{4,20},{5,21},{6,22},{7,23},{8,24},{9,... | collective-permute-start | bytes 1327112 | tf_op jit(solution)/shard_map/ppermute | solution.py:20
  22.8 12.0 %collective-permute-start.4 = (bf16[1,96,1536]{2,1,0:T(8,128)(2,1)S(1)}, bf16[1,96,1536]{2,1,0:T(8,128)(2,1)S(1)}, u32[]{:S(2)}, u32[]{:S(2)}) collective-permute-start(bf16[1,96,1536]{2,1,0:T(8,128)(2,1)S(1)} %constant_dynamic-slice_fusion.1), channel_id=1, source_target_pairs={{0,12},{1,13},{2,14},{3,15},{4,8},{5,9},{6,10},{7,11},{8,4},{9,5},... | collective-permute-start | bytes 884744 | tf_op jit(solution)/shard_map/ppermute | solution.py:20
  25.1 11.7 %collective-permute-start.5 = (bf16[1,96,1536]{2,1,0:T(8,128)(2,1)S(1)}, bf16[1,96,1536]{2,1,0:T(8,128)(2,1)S(1)}, u32[]{:S(2)}, u32[]{:S(2)}) collective-permute-start(bf16[1,96,1536]{2,1,0:T(8,128)(2,1)S(1)} %constant_dynamic-slice_fusion.1), channel_id=1, source_target_pairs={{0,4},{1,5},{2,6},{3,7},{4,0},{5,1},{6,2},{7,3},{8,12},{9,13},{10,... | collective-permute-start | bytes 884744 | tf_op jit(solution)/shard_map/ppermute | solution.py:20
  33.3 11.8 %collective-permute-start.8 = (bf16[3,96,768]{2,1,0:T(8,128)(2,1)S(1)}, bf16[3,96,768]{2,1,0:T(8,128)(2,1)S(1)}, u32[]{:S(2)}, u32[]{:S(2)}) collective-permute-start(bf16[3,96,768]{2,1,0:T(8,128)(2,1)S(1)} %collective-permute-done.3.refs_1_), channel_id=1, source_target_pairs={{0,16},{1,17},{2,18},{3,19},{4,20},{5,21},{6,22},{7,23},{8,24},{9,... | collective-permute-start | bytes 1327112 | tf_op jit(solution)/shard_map/ppermute | solution.py:20
  36.8 7.8 %collective-permute-start.9 = (bf16[1,96,1536]{2,1,0:T(8,128)(2,1)S(1)}, bf16[1,96,1536]{2,1,0:T(8,128)(2,1)S(1)}, u32[]{:S(2)}, u32[]{:S(2)}) collective-permute-start(bf16[1,96,1536]{2,1,0:T(8,128)(2,1)S(1)} %collective-permute-done.4), channel_id=1, source_target_pairs={{0,4},{1,5},{2,6},{3,7},{4,0},{5,1},{6,2},{7,3},{8,12},{9,13},{10,... | collective-permute-start | bytes 884744 | tf_op jit(solution)/shard_map/ppermute | solution.py:20
  37.5 7.6 %collective-permute-start.10 = (bf16[1,96,1536]{2,1,0:T(8,128)(2,1)S(1)}, bf16[1,96,1536]{2,1,0:T(8,128)(2,1)S(1)}, u32[]{:S(2)}, u32[]{:S(2)}) collective-permute-start(bf16[1,96,1536]{2,1,0:T(8,128)(2,1)S(1)} %collective-permute-done.5), channel_id=1, source_target_pairs={{0,2},{1,3},{2,0},{3,1},{4,6},{5,7},{6,4},{7,5},{8,10},{9,11},{10,... | collective-permute-start | bytes 884744 | tf_op jit(solution)/shard_map/ppermute | solution.py:20
  38.1 1.1 %copy-start.3 = (bf16[1536,256]{1,0:T(8,128)(2,1)S(1)}, bf16[1536,256]{1,0:T(8,128)(2,1)}, u32[]{:S(2)}) copy-start(bf16[1536,256]{1,0:T(8,128)(2,1)} %get-tuple-element.80.refs_6_.refs_8_) | copy-start | bytes 2359300
  45.3 3.8 %copy-start.4 = (bf16[1536,256]{1,0:T(8,128)(2,1)S(1)}, bf16[1536,256]{1,0:T(8,128)(2,1)}, u32[]{:S(2)}) copy-start(bf16[1536,256]{1,0:T(8,128)(2,1)} %get-tuple-element.80.refs_6_.refs_8_) | copy-start | bytes 2359300
  45.3 3.8 %collective-permute-start.11 = (bf16[4,3,96,768]{3,2,1,0:T(8,128)(2,1)S(1)}, bf16[4,3,96,768]{3,2,1,0:T(8,128)(2,1)S(1)}, u32[]{:S(2)}, u32[]{:S(2)}) collective-permute-start(bf16[4,3,96,768]{3,2,1,0:T(8,128)(2,1)S(1)} %stack.18.refs_2_.refs_3_), channel_id=1, source_target_pairs={{0,1},{1,0},{2,3},{3,2},{4,5},{5,4},{6,7},{7,6},{8,9},{9,8},{10,11... | collective-permute-start | bytes 5308424 | tf_op jit(solution)/shard_map/ppermute | solution.py:20
  45.4 6.5 %collective-permute-start.12 = (bf16[4,96,1536]{2,1,0:T(8,128)(2,1)S(1)}, bf16[4,96,1536]{2,1,0:T(8,128)(2,1)S(1)}, u32[]{:S(2)}, u32[]{:S(2)}) collective-permute-start(bf16[4,96,1536]{2,1,0:T(8,128)(2,1)S(1)} %stack.19.refs_0_), channel_id=1, source_target_pairs={{0,1},{1,0},{2,3},{3,2},{4,5},{5,4},{6,7},{7,6},{8,9},{9,8},{10,11... | collective-permute-start | bytes 3538952 | tf_op jit(solution)/shard_map/ppermute | solution.py:20
  46.0 15.5 %collective-permute-start.13 = (bf16[384,768]{1,0:T(8,128)(2,1)}, bf16[384,768]{1,0:T(8,128)(2,1)S(1)}, u32[]{:S(2)}, u32[]{:S(2)}) collective-permute-start(bf16[384,768]{1,0:T(8,128)(2,1)} %collective-permute-done.6.refs_0_), channel_id=1, source_target_pairs={{0,16},{1,17},{2,18},{3,19},{4,20},{5,21},{6,22},{7,23},{8,24},{9,... | collective-permute-start | bytes 1769480 | tf_op jit(solution)/shard_map/ppermute | solution.py:20
  46.5 12.7 %collective-permute-start.15 = (bf16[1,96,1536]{2,1,0:T(8,128)(2,1)S(1)}, bf16[1,96,1536]{2,1,0:T(8,128)(2,1)S(1)}, u32[]{:S(2)}, u32[]{:S(2)}) collective-permute-start(bf16[1,96,1536]{2,1,0:T(8,128)(2,1)S(1)} %collective-permute-done.4), channel_id=1, source_target_pairs={{0,2},{1,3},{2,0},{3,1},{4,6},{5,7},{6,4},{7,5},{8,10},{9,11},{10,... | collective-permute-start | bytes 884744 | tf_op jit(solution)/shard_map/ppermute | solution.py:20
  47.4 14.2 %collective-permute-start.14 = (bf16[1,96,1536]{2,1,0:T(8,128)(2,1)S(1)}, bf16[1,96,1536]{2,1,0:T(8,128)(2,1)S(1)}, u32[]{:S(2)}, u32[]{:S(2)}) collective-permute-start(bf16[1,96,1536]{2,1,0:T(8,128)(2,1)S(1)} %collective-permute-done.9), channel_id=1, source_target_pairs={{0,2},{1,3},{2,0},{3,1},{4,6},{5,7},{6,4},{7,5},{8,10},{9,11},{10,... | collective-permute-start | bytes 884744 | tf_op jit(solution)/shard_map/ppermute | solution.py:20
  61.6 3.1 %collective-permute-start.16 = (bf16[2,96,1536]{2,1,0:T(8,128)(2,1)S(1)}, bf16[2,96,1536]{2,1,0:T(8,128)(2,1)S(1)}, u32[]{:S(2)}, u32[]{:S(2)}) collective-permute-start(bf16[2,96,1536]{2,1,0:T(8,128)(2,1)S(1)} %stack.20.refs_0_), channel_id=1, source_target_pairs={{0,1},{1,0},{2,3},{3,2},{4,5},{5,4},{6,7},{7,6},{8,9},{9,8},{10,11... | collective-permute-start | bytes 1769480 | tf_op jit(solution)/shard_map/ppermute | solution.py:20
  64.6 2.9 %copy-start.2 = (bf16[384,1536]{1,0:T(8,128)(2,1)S(1)}, bf16[384,1536]{1,0:T(8,128)(2,1)}, u32[]{:S(2)}) copy-start(bf16[384,1536]{1,0:T(8,128)(2,1)} %wo0.1) | copy-start | bytes 3538948
  67.6 3.9 %collective-permute-start.18 = (bf16[384,1536]{1,0:T(8,128)(2,1)S(1)}, bf16[384,1536]{1,0:T(8,128)(2,1)S(1)}, u32[]{:S(2)}, u32[]{:S(2)}) collective-permute-start(bf16[384,1536]{1,0:T(8,128)(2,1)S(1)} %copy-done.2), channel_id=1, source_target_pairs={{0,1},{1,0},{2,3},{3,2},{4,5},{5,4},{6,7},{7,6},{8,9},{9,8},{10,11... | collective-permute-start | bytes 3538952 | tf_op jit(solution)/shard_map/ppermute | solution.py:20
  68.1 3.3 %collective-permute-start.17 = (bf16[2,2,192,384]{3,2,1,0:T(8,128)(2,1)S(1)}, bf16[2,2,192,384]{3,2,1,0:T(8,128)(2,1)S(1)}, u32[]{:S(2)}, u32[]{:S(2)}) collective-permute-start(bf16[2,2,192,384]{3,2,1,0:T(8,128)(2,1)S(1)} %get-tuple-element.117), channel_id=1, source_target_pairs={{0,1},{1,0},{2,3},{3,2},{4,5},{5,4},{6,7},{7,6},{8,9},{9,8},{10,11... | collective-permute-start | bytes 1769480 | tf_op jit(solution)/shard_map/ppermute | solution.py:20
  68.2 9.4 %collective-permute-start.19 = (bf16[2,192,384]{2,1,0:T(8,128)(2,1)S(1)}, bf16[2,192,384]{2,1,0:T(8,128)(2,1)S(1)}, u32[]{:S(2)}, u32[]{:S(2)}) collective-permute-start(bf16[2,192,384]{2,1,0:T(8,128)(2,1)S(1)} %get-tuple-element.115.att0), channel_id=1, source_target_pairs={{0,2},{1,3},{2,0},{3,1},{4,6},{5,7},{6,4},{7,5},{8,10},{9,11},{10,... | collective-permute-start | bytes 884744 | tf_op jit(solution)/shard_map/ppermute | solution.py:20
  72.9 5.6 %copy-start.10 = (f32[1536]{0:T(1024)S(1)}, f32[1536]{0:T(1024)}, u32[]{:S(2)}) copy-start(f32[1536]{0:T(1024)} %param.17) | copy-start | bytes 18436
  72.9 6.7 %copy-start.6 = (bf16[1536,768]{1,0:T(8,128)(2,1)S(1)}, bf16[1536,768]{1,0:T(8,128)(2,1)}, u32[]{:S(2)}) copy-start(bf16[1536,768]{1,0:T(8,128)(2,1)} %refs_2_.3) | copy-start | bytes 7077892
  72.9 6.7 %copy-start.7 = (bf16[768,1536]{1,0:T(8,128)(2,1)S(1)}, bf16[768,1536]{1,0:T(8,128)(2,1)}, u32[]{:S(2)}) copy-start(bf16[768,1536]{1,0:T(8,128)(2,1)} %refs_3_.5) | copy-start | bytes 7077892
  74.3 5.3 %collective-permute-start.21 = (bf16[384,768]{1,0:T(8,128)(2,1)}, bf16[384,768]{1,0:T(8,128)(2,1)S(1)}, u32[]{:S(2)}, u32[]{:S(2)}) collective-permute-start(bf16[384,768]{1,0:T(8,128)(2,1)} %collective-permute-done.6.refs_0_), channel_id=1, source_target_pairs={{0,1},{1,0},{2,3},{3,2},{4,5},{5,4},{6,7},{7,6},{8,9},{9,8},{10,11... | collective-permute-start | bytes 1769480 | tf_op jit(solution)/shard_map/ppermute | solution.py:20
  74.8 4.8 %collective-permute-start.22 = (bf16[384,768]{1,0:T(8,128)(2,1)S(1)}, bf16[384,768]{1,0:T(8,128)(2,1)S(1)}, u32[]{:S(2)}, u32[]{:S(2)}) collective-permute-start(bf16[384,768]{1,0:T(8,128)(2,1)S(1)} %collective-permute-done.13.refs_8_), channel_id=1, source_target_pairs={{0,1},{1,0},{2,3},{3,2},{4,5},{5,4},{6,7},{7,6},{8,9},{9,8},{10,11... | collective-permute-start | bytes 1769480 | tf_op jit(solution)/shard_map/ppermute | solution.py:20
  77.6 2.0 %collective-permute-start.20 = (bf16[2,192,384]{2,1,0:T(8,128)(2,1)S(1)}, bf16[2,192,384]{2,1,0:T(8,128)(2,1)S(1)}, u32[]{:S(2)}, u32[]{:S(2)}) collective-permute-start(bf16[2,192,384]{2,1,0:T(8,128)(2,1)S(1)} %collective-permute-done.19.refs_4_), channel_id=1, source_target_pairs={{0,1},{1,0},{2,3},{3,2},{4,5},{5,4},{6,7},{7,6},{8,9},{9,8},{10,11... | collective-permute-start | bytes 884744 | tf_op jit(solution)/shard_map/ppermute | solution.py:20
  77.6 9.4 %collective-permute-start.23 = (bf16[2,192,384]{2,1,0:T(8,128)(2,1)S(1)}, bf16[2,192,384]{2,1,0:T(8,128)(2,1)S(1)}, u32[]{:S(2)}, u32[]{:S(2)}) collective-permute-start(bf16[2,192,384]{2,1,0:T(8,128)(2,1)S(1)} %get-tuple-element.119.att0), channel_id=1, source_target_pairs={{0,2},{1,3},{2,0},{3,1},{4,6},{5,7},{6,4},{7,5},{8,10},{9,11},{10,... | collective-permute-start | bytes 884744 | tf_op jit(solution)/shard_map/ppermute | solution.py:20
  87.0 1.6 %collective-permute-start.24 = (bf16[2,192,384]{2,1,0:T(8,128)(2,1)S(1)}, bf16[2,192,384]{2,1,0:T(8,128)(2,1)S(1)}, u32[]{:S(2)}, u32[]{:S(2)}) collective-permute-start(bf16[2,192,384]{2,1,0:T(8,128)(2,1)S(1)} %get-tuple-element.134), channel_id=1, source_target_pairs={{0,1},{1,0},{2,3},{3,2},{4,5},{5,4},{6,7},{7,6},{8,9},{9,8},{10,11... | collective-permute-start | bytes 884744 | tf_op jit(solution)/shard_map/ppermute | solution.py:20
  87.0 2.6 %collective-permute-start.25 = (bf16[2,192,384]{2,1,0:T(8,128)(2,1)S(1)}, bf16[2,192,384]{2,1,0:T(8,128)(2,1)S(1)}, u32[]{:S(2)}, u32[]{:S(2)}) collective-permute-start(bf16[2,192,384]{2,1,0:T(8,128)(2,1)S(1)} %collective-permute-done.23.refs_4_), channel_id=1, source_target_pairs={{0,1},{1,0},{2,3},{3,2},{4,5},{5,4},{6,7},{7,6},{8,9},{9,8},{10,11... | collective-permute-start | bytes 884744 | tf_op jit(solution)/shard_map/ppermute | solution.py:20
  88.7 6.0 %collective-permute-start.26 = (bf16[192,384]{1,0:T(8,128)(2,1)S(1)}, bf16[192,384]{1,0:T(8,128)(2,1)S(1)}, u32[]{:S(2)}, u32[]{:S(2)}) collective-permute-start(bf16[192,384]{1,0:T(8,128)(2,1)S(1)} %fusion.8), channel_id=1, source_target_pairs={{0,2},{1,3},{2,0},{3,1},{4,6},{5,7},{6,4},{7,5},{8,10},{9,11},{10,... | collective-permute-start | bytes 442376 | tf_op jit(solution)/shard_map/ppermute | solution.py:20
  94.6 1.6 %collective-permute-start.27 = (bf16[2,192,384]{2,1,0:T(8,128)(2,1)S(1)}, bf16[2,192,384]{2,1,0:T(8,128)(2,1)S(1)}, u32[]{:S(2)}, u32[]{:S(2)}) collective-permute-start(bf16[2,192,384]{2,1,0:T(8,128)(2,1)S(1)} %get-tuple-element.144), channel_id=1, source_target_pairs={{0,1},{1,0},{2,3},{3,2},{4,5},{5,4},{6,7},{7,6},{8,9},{9,8},{10,11... | collective-permute-start | bytes 884744 | tf_op jit(solution)/shard_map/ppermute | solution.py:20
  96.3 6.0 %collective-permute-start.28 = (bf16[192,384]{1,0:T(8,128)(2,1)S(1)}, bf16[192,384]{1,0:T(8,128)(2,1)S(1)}, u32[]{:S(2)}, u32[]{:S(2)}) collective-permute-start(bf16[192,384]{1,0:T(8,128)(2,1)S(1)} %fusion.9), channel_id=1, source_target_pairs={{0,2},{1,3},{2,0},{3,1},{4,6},{5,7},{6,4},{7,5},{8,10},{9,11},{10,... | collective-permute-start | bytes 442376 | tf_op jit(solution)/shard_map/ppermute | solution.py:20
where the time goes:
time: 103 us
  waiting for transfers between devices  33.7 us (33%)
  Pallas kernels  33.3 us (32%)
  starting transfers between devices  25.8 us (25%)
  local copies, waits for them, and re-layouts  5.82 us (6%)
  other arithmetic  4.18 us (4%)
    ppermute x29, waiting for transfers between devices, swap(): lax.ppermute(block, AXES, [(i, i ^ code) for i in range(groups * seq * mp)])  33.7 us
    ppermute x29, starting transfers between devices, swap(): lax.ppermute(block, AXES, [(i, i ^ code) for i in range(groups * seq * mp)])  25.8 us
    pallas_call x5, Pallas kernels, chunk_call(): pl.pallas_call(functools.partial(chunk_kernel, dims, batches, where, last...  18.5 us
    pallas_call x2, Pallas kernels, mid_call(): pl.pallas_call(functools.partial(mid_kernel, groups), out_shape=[jax.Shap...  9.73 us
    pallas_call x2, Pallas kernels, mix_call(): pl.pallas_call(functools.partial(mix_kernel, n), out_shape=jax.ShapeDtype...  2.8 us
    convert_element_type x1, other arithmetic, shards(): (gain * w.astype(f32)).astype(bf16)  2.75 us
    pallas_call x5, Pallas kernels, stack_call(): pl.pallas_call(stack_kernel, out_shape=jax.ShapeDtypeStruct(shape, arrays...  2.28 us
  transfers between devices with their start and end apart: 29, of which 14 were waited for; matrix products, arithmetic and copies ran while one was open for 6% of the time, Pallas kernels for 29%

commit v1 on v0

--- a/solution.py
+++ b/solution.py
@@ -180,7 +180,11 @@
     )(scal, *args)
 
 
-def mix_kernel(n, x_ref, loc_ref, back_ref, att0, att1, wo0, wo1, out_ref):
+def mix_kernel(n, x_ref, loc_ref, back_ref, att0, att1, wo0, wo1, *refs):
+    count = len(refs) // 2
+    out_ref = refs[count]
+    for i in range(count):
+        refs[count + 1 + i][...] = refs[i][...]
     rows = out_ref.shape[1]
     lo = n * rows
     mixed = dot(att0[...].reshape(2 * rows, -1), wo0[...]) + dot(att1[n].reshape(2 * rows, -1), wo1[...])
@@ -189,19 +193,19 @@
         out_ref[t] = x_f + loc[lo : lo + rows].astype(f32) + mixed[t * rows : (t + 1) * rows]
 
 
-def mix_call(n, x, loc, back, att, wo):
+def mix_call(n, x, loc, back, att, wo, copied=()):
     rows, width = att[0].shape[1], x.shape[1]
     return pl.pallas_call(
         functools.partial(mix_kernel, n),
-        out_shape=jax.ShapeDtypeStruct((2, rows, width), f32),
-        in_specs=[VMEM] * 7,
-        out_specs=VMEM,
+        out_shape=[jax.ShapeDtypeStruct((2, rows, width), f32)] + [jax.ShapeDtypeStruct(a.shape, a.dtype) for a in copied],
+        in_specs=[VMEM] * (7 + len(copied)),
+        out_specs=[VMEM] * (1 + len(copied)),
         compiler_params=pltpu.CompilerParams(vmem_limit_bytes=24 * 2**20),
         cost_estimate=pl.CostEstimate(
             flops=8 * rows * width * wo[0].shape[0], bytes_accessed=8 * 2**20, transcendentals=0
         ),
         name="mix",
-    )(x, loc, back, *att, *wo)
+    )(x, loc, back, *att, *wo, *copied)
 
 
 def mid_kernel(groups, scal, *refs):
@@ -396,14 +400,14 @@
 
     far0 = over_x(a0)
     blocks_odd = swap(blocks, m=1)
-    part0 = mix_call(0, *stream, [a0, blocks_odd], wo_own)
+    (part0,) = mix_call(0, *stream, [a0, blocks_odd], wo_own)
     far1 = over_x(a1)
-    part1 = mix_call(1, *stream, [a1, blocks_odd], wo_own)
+    part1, *copies = mix_call(1, *stream, [a1, blocks_odd], wo_own, mix_far[: nx - 1])
     part0, part1, mix_far = together(part0, part1, mix_far)
     wo_far = []
     for h in range(groups):
         some = mix_far[h * (nx - 1) : (h + 1) * (nx - 1)]
-        wo_far += [*(a if h else stack_call([a])[0] for a in some), *(swap(a, m=1) for a in some)]
+        wo_far += [*(some if h else copies), *(swap(a, m=1) for a in some)]
     part0, part1, *far0 = together(part0, part1, *far0)
     even0, odd0, share0 = mid_call(groups, mp, scal, part0, *w_mid, cores(far0), wo_far)
     even0, odd0, share0, *far1 = together(even0, odd0, share0, *far1)

time: 103 us -> 103 us (level)
    pallas_call x2, Pallas kernels: 2.8 us -> 4.07 us  [mix_call(): pl.pallas_call(functools.partial(mix_kernel, n), out_shape=[jax.ShapeDtyp...]
    pallas_call x5 -> x4, Pallas kernels: 2.28 us -> 1.17 us  [stack_call(): pl.pallas_call(stack_kernel, out_shape=jax.ShapeDtypeStruct(shape, arrays...]
  transfers between devices with their start and end apart: 29 -> 29, of which waited for: 14 -> 15; matrix products, arithmetic and copies ran while one was open for 6% -> 6% of each run, Pallas kernels for 29% -> 29%
where the time goes in v1:
time: 103 us
  waiting for transfers between devices  33.6 us (33%)
  Pallas kernels  33.5 us (33%)
  starting transfers between devices  25.8 us (25%)
  local copies, waits for them, and re-layouts  5.81 us (6%)
  other arithmetic  4.19 us (4%)
    ppermute x29, waiting for transfers between devices, swap(): lax.ppermute(block, AXES, [(i, i ^ code) for i in range(groups * seq * mp)])  33.6 us
    ppermute x29, starting transfers between devices, swap(): lax.ppermute(block, AXES, [(i, i ^ code) for i in range(groups * seq * mp)])  25.8 us
    pallas_call x5, Pallas kernels, chunk_call(): pl.pallas_call(functools.partial(chunk_kernel, dims, batches, where, last...  18.5 us
    pallas_call x2, Pallas kernels, mid_call(): pl.pallas_call(functools.partial(mid_kernel, groups), out_shape=[jax.Shap...  9.73 us
    pallas_call x2, Pallas kernels, mix_call(): pl.pallas_call(functools.partial(mix_kernel, n), out_shape=[jax.ShapeDtyp...  4.07 us
    convert_element_type x1, other arithmetic, shards(): (gain * w.astype(f32)).astype(bf16)  2.75 us
  transfers between devices with their start and end apart: 29, of which 15 were waited for; matrix products, arithmetic and copies ran while one was open for 6% of the time, Pallas kernels for 29%

profile of v1, /device:TPU:0, one launch (start us, length us, event | category | flops | bytes accessed | tf_op | source)
XLA Modules:
  0.0 103.2 jit_solution(3559949321967649941)
XLA Ops:
  0.0 1.6 %dynamic_slice.9 = bf16[96,768]{1,0:T(8,128)(2,1)} dynamic-slice(bf16[384,1536]{1,0:T(8,128)(2,1)} %loc_ref.3, s32[]{:T(128)S(6)} %select_n.10, s32[]{:T(128)S(6)} %select_n.11), dynamic_slice_sizes={96,768} | dynamic-slice | bytes 294916 | tf_op jit(solution)/shard_map/dynamic_slice | solution.py:336
  1.6 3.0 %collective-permute-start = (bf16[96,768]{1,0:T(8,128)(2,1)}, bf16[96,768]{1,0:T(8,128)(2,1)S(1)}, u32[]{:S(2)}, u32[]{:S(2)}) collective-permute-start(bf16[96,768]{1,0:T(8,128)(2,1)} %dynamic_slice.9), channel_id=1, source_target_pairs={{0,4},{1,5},{2,6},{3,7},{4,0},{5,1},{6,2},{7,3},{8,12},{9,13},{10,... | collective-permute-start | bytes 442376 | tf_op jit(solution)/shard_map/ppermute | solution.py:20
  4.6 2.6 %collective-permute-start.1 = (bf16[96,768]{1,0:T(8,128)(2,1)}, bf16[96,768]{1,0:T(8,128)(2,1)S(1)}, u32[]{:S(2)}, u32[]{:S(2)}) collective-permute-start(bf16[96,768]{1,0:T(8,128)(2,1)} %dynamic_slice.9), channel_id=1, source_target_pairs={{0,8},{1,9},{2,10},{3,11},{4,12},{5,13},{6,14},{7,15},{8,0},{9,1},... | collective-permute-start | bytes 442376 | tf_op jit(solution)/shard_map/ppermute | solution.py:20
  7.2 1.9 %constant_dynamic-slice_fusion = bf16[384,768]{1,0:T(8,128)(2,1)} fusion(bf16[384,1536]{1,0:T(8,128)(2,1)} %wo0.1, s32[]{:T(128)S(6)} %select_n.11), kind=kLoop, calls=%fused_computation.22 | loop fusion | bytes 1179652 | tf_op jit(solution)/shard_map/dynamic_slice | solution.py:338
  9.1 1.7 %collective-permute-start.6 = (bf16[384,768]{1,0:T(8,128)(2,1)}, bf16[384,768]{1,0:T(8,128)(2,1)}, u32[]{:S(2)}, u32[]{:S(2)}) collective-permute-start(bf16[384,768]{1,0:T(8,128)(2,1)} %constant_dynamic-slice_fusion), channel_id=1, source_target_pairs={{0,2},{1,3},{2,0},{3,1},{4,6},{5,7},{6,4},{7,5},{8,10},{9,11},{10,... | collective-permute-start | bytes 1769480 | tf_op jit(solution)/shard_map/ppermute | solution.py:20
  10.8 2.7 %fusion = (bf16[1536,256]{1,0:T(8,128)(2,1)S(1)}, bf16[1536,256]{1,0:T(8,128)(2,1)}) fusion(bf16[2,1536,256]{2,1,0:T(8,128)(2,1)} %param.13, f32[1536]{0:T(1024)} %param.12), kind=kLoop, calls=%fused_computation.2 | loop fusion | flops 2359296 | bytes 3151872 | tf_op jit(solution)/shard_map/convert_element_type | solution.py:314
  13.6 0.3 multiply_convert_fusion.refs_5_.refs_7_.refs_8_
  13.9 1.1 %constant_dynamic-slice_fusion.1 = bf16[1,96,1536]{2,1,0:T(8,128)(2,1)S(1)} fusion(bf16[4,96,1536]{2,1,0:T(8,128)(2,1)} %bitcast.40, s32[]{:T(128)S(6)} %select_n.12), kind=kLoop, calls=%fused_computation.23 | loop fusion | bytes 589828 | tf_op jit(solution)/shard_map/dynamic_slice | solution.py:341
  15.0 3.8 %collective-permute-done.1.refs_1_ = bf16[96,768]{1,0:T(8,128)(2,1)S(1)} collective-permute-done((bf16[96,768]{1,0:T(8,128)(2,1)}, bf16[96,768]{1,0:T(8,128)(2,1)S(1)}, u32[]{:S(2)}, u32[]{:S(2)}) %collective-permute-start.1) | collective-permute-done | bytes 147488 | tf_op jit(solution)/shard_map/ppermute | solution.py:20
  18.8 0.9 stack.16.refs_0_
  19.7 1.6 %collective-permute-start.3 = (bf16[3,96,768]{2,1,0:T(8,128)(2,1)S(1)}, bf16[3,96,768]{2,1,0:T(8,128)(2,1)S(1)}, u32[]{:S(2)}, u32[]{:S(2)}) collective-permute-start(bf16[3,96,768]{2,1,0:T(8,128)(2,1)S(1)} %stack.16.refs_0_), channel_id=1, source_target_pairs={{0,2},{1,3},{2,0},{3,1},{4,6},{5,7},{6,4},{7,5},{8,10},{9,11},{10,... | collective-permute-start | bytes 1327112 | tf_op jit(solution)/shard_map/ppermute | solution.py:20
  21.3 1.5 %collective-permute-start.7 = (bf16[3,96,768]{2,1,0:T(8,128)(2,1)S(1)}, bf16[3,96,768]{2,1,0:T(8,128)(2,1)S(1)}, u32[]{:S(2)}, u32[]{:S(2)}) collective-permute-start(bf16[3,96,768]{2,1,0:T(8,128)(2,1)S(1)} %stack.16.refs_0_), channel_id=1, source_target_pairs={{0,16},{1,17},{2,18},{3,19},{4,20},{5,21},{6,22},{7,23},{8,24},{9,... | collective-permute-start | bytes 1327112 | tf_op jit(solution)/shard_map/ppermute | solution.py:20
  22.8 2.3 %collective-permute-start.4 = (bf16[1,96,1536]{2,1,0:T(8,128)(2,1)S(1)}, bf16[1,96,1536]{2,1,0:T(8,128)(2,1)S(1)}, u32[]{:S(2)}, u32[]{:S(2)}) collective-permute-start(bf16[1,96,1536]{2,1,0:T(8,128)(2,1)S(1)} %constant_dynamic-slice_fusion.1), channel_id=1, source_target_pairs={{0,12},{1,13},{2,14},{3,15},{4,8},{5,9},{6,10},{7,11},{8,4},{9,5},... | collective-permute-start | bytes 884744 | tf_op jit(solution)/shard_map/ppermute | solution.py:20
  25.1 1.7 %collective-permute-start.5 = (bf16[1,96,1536]{2,1,0:T(8,128)(2,1)S(1)}, bf16[1,96,1536]{2,1,0:T(8,128)(2,1)S(1)}, u32[]{:S(2)}, u32[]{:S(2)}) collective-permute-start(bf16[1,96,1536]{2,1,0:T(8,128)(2,1)S(1)} %constant_dynamic-slice_fusion.1), channel_id=1, source_target_pairs={{0,4},{1,5},{2,6},{3,7},{4,0},{5,1},{6,2},{7,3},{8,12},{9,13},{10,... | collective-permute-start | bytes 884744 | tf_op jit(solution)/shard_map/ppermute | solution.py:20
  26.8 6.5 %collective-permute-done.3.refs_1_ = bf16[3,96,768]{2,1,0:T(8,128)(2,1)S(1)} collective-permute-done((bf16[3,96,768]{2,1,0:T(8,128)(2,1)S(1)}, bf16[3,96,768]{2,1,0:T(8,128)(2,1)S(1)}, u32[]{:S(2)}, u32[]{:S(2)}) %collective-permute-start.3) | collective-permute-done | bytes 442400 | tf_op jit(solution)/shard_map/ppermute | solution.py:20
  33.3 1.5 %collective-permute-start.8 = (bf16[3,96,768]{2,1,0:T(8,128)(2,1)S(1)}, bf16[3,96,768]{2,1,0:T(8,128)(2,1)S(1)}, u32[]{:S(2)}, u32[]{:S(2)}) collective-permute-start(bf16[3,96,768]{2,1,0:T(8,128)(2,1)S(1)} %collective-permute-done.3.refs_1_), channel_id=1, source_target_pairs={{0,16},{1,17},{2,18},{3,19},{4,20},{5,21},{6,22},{7,23},{8,24},{9,... | collective-permute-start | bytes 1327112 | tf_op jit(solution)/shard_map/ppermute | solution.py:20
  34.8 2.0 %collective-permute-done.5 = bf16[1,96,1536]{2,1,0:T(8,128)(2,1)S(1)} collective-permute-done((bf16[1,96,1536]{2,1,0:T(8,128)(2,1)S(1)}, bf16[1,96,1536]{2,1,0:T(8,128)(2,1)S(1)}, u32[]{:S(2)}, u32[]{:S(2)}) %collective-permute-start.5) | collective-permute-done | bytes 294944 | tf_op jit(solution)/shard_map/ppermute | solution.py:20
  36.8 0.7 collective-permute-start.9
  37.5 0.5 collective-permute-start.10
  38.0 0.1 pad_add_fusion.scal
  38.1 1.1 %copy-done.3 = bf16[1536,256]{1,0:T(8,128)(2,1)S(1)} copy-done((bf16[1536,256]{1,0:T(8,128)(2,1)S(1)}, bf16[1536,256]{1,0:T(8,128)(2,1)}, u32[]{:S(2)}) %copy-start.3) | copy-done | bytes 786456
  39.3 2.5 %own_forward.1 = (f32[2,384,256]{2,1,0:T(8,128)S(1)}, bf16[384,256]{1,0:T(8,128)(2,1)S(1)}) custom-call(s32[2]{0:T(128)S(1)} %pad_add_fusion.scal, bf16[4,96,1536]{2,1,0:T(8,128)(2,1)S(1)} %bitcast.41, bf16[4,96,1536]{2,1,0:T(8,128)(2,1)S(1)} %bitcast.35, bf16[192,192]{1,0:T(8,128)(2,1)S(1)} %fusion.7.refs_2_.refs_4_.refs_5_, f32[2]{0:T(128)S(1)} %copy-done.5, ...), custom_call_target="tpu_custom_call" | custom-call | flops 1048576 | bytes 1048576 | tf_op jit(solution)/shard_map/own_forward/pallas_call | solution.py:171
  41.8 2.8 %collective-permute-done.9 = bf16[1,96,1536]{2,1,0:T(8,128)(2,1)S(1)} collective-permute-done((bf16[1,96,1536]{2,1,0:T(8,128)(2,1)S(1)}, bf16[1,96,1536]{2,1,0:T(8,128)(2,1)S(1)}, u32[]{:S(2)}, u32[]{:S(2)}) %collective-permute-start.9) | collective-permute-done | bytes 294944 | tf_op jit(solution)/shard_map/ppermute | solution.py:20
  44.6 0.5 collective-permute-done.10
  45.1 0.1 stack.17.refs_2_.refs_3_
  45.3 0.1 collective-permute-start.11
  45.3 0.1 stack.18.refs_0_
  45.4 0.6 collective-permute-start.12
  46.0 0.5 collective-permute-start.13
  46.5 0.9 collective-permute-start.15
  47.4 1.1 %collective-permute-start.14 = (bf16[1,96,1536]{2,1,0:T(8,128)(2,1)S(1)}, bf16[1,96,1536]{2,1,0:T(8,128)(2,1)S(1)}, u32[]{:S(2)}, u32[]{:S(2)}) collective-permute-start(bf16[1,96,1536]{2,1,0:T(8,128)(2,1)S(1)} %collective-permute-done.9), channel_id=1, source_target_pairs={{0,2},{1,3},{2,0},{3,1},{4,6},{5,7},{6,4},{7,5},{8,10},{9,11},{10,... | collective-permute-start | bytes 884744 | tf_op jit(solution)/shard_map/ppermute | solution.py:20
  48.5 0.5 collective-permute-done.11.refs_3_.refs_4_
  49.0 2.9 %own_back.1 = (f32[2,384,256]{2,1,0:T(8,128)S(1)}, bf16[384,256]{1,0:T(8,128)(2,1)S(1)}, bf16[4,96,1536]{2,1,0:T(8,128)(2,1)S(1)}) custom-call(s32[2]{0:T(128)S(1)} %pad_add_fusion.scal, bf16[4,96,1536]{2,1,0:T(8,128)(2,1)S(1)} %bitcast.42, bf16[4,96,1536]{2,1,0:T(8,128)(2,1)S(1)} %bitcast.36, bf16[4,3,96,768]{3,2,1,0:T(8,128)(2,1)S(1)} %stack.17.refs_2_.refs_3_, ...), custom_call_target="tpu_custom_call" | custom-call | flops 1048576 | bytes 1048576 | tf_op jit(solution)/shard_map/own_back/pallas_call | solution.py:171
  51.9 7.2 %first.1 = (f32[2,384,256]{2,1,0:T(8,128)S(1)}, f32[2,384,256]{2,1,0:T(8,128)S(1)}) custom-call(s32[2]{0:T(128)S(1)} %pad_add_fusion.scal, bf16[4,96,1536]{2,1,0:T(8,128)(2,1)S(1)} %stack.18.refs_0_, bf16[4,96,1536]{2,1,0:T(8,128)(2,1)S(1)} %collective-permute-done.12.refs_1_, bf16[4,96,1536]{2,1,0:T(8,128)(2,1)S(1)} %bitcast.37, ...), custom_call_target="tpu_custom_call" | custom-call | flops 1048576 | bytes 1048576 | tf_op jit(solution)/shard_map/first/pallas_call | solution.py:171
  59.2 2.3 %collective-permute-done.13.refs_8_ = bf16[384,768]{1,0:T(8,128)(2,1)S(1)} collective-permute-done((bf16[384,768]{1,0:T(8,128)(2,1)}, bf16[384,768]{1,0:T(8,128)(2,1)S(1)}, u32[]{:S(2)}, u32[]{:S(2)}) %collective-permute-start.13) | collective-permute-done | bytes 589856 | tf_op jit(solution)/shard_map/ppermute | solution.py:20
  61.5 0.0 collective-permute-done.14
  61.6 0.1 collective-permute-start.16
  61.6 3.0 %second.1 = (f32[2,384,256]{2,1,0:T(8,128)S(1)}, f32[2,384,256]{2,1,0:T(8,128)S(1)}) custom-call(s32[2]{0:T(128)S(1)} %pad_add_fusion.scal, bf16[2,96,1536]{2,1,0:T(8,128)(2,1)S(1)} %stack.19.refs_0_, bf16[4,96,1536]{2,1,0:T(8,128)(2,1)S(1)} %bitcast.38, bf16[4,3,96,768]{3,2,1,0:T(8,128)(2,1)S(1)} %stack.17.refs_2_.refs_3_, ...), custom_call_target="tpu_custom_call" | custom-call | flops 1048576 | bytes 1048576 | tf_op jit(solution)/shard_map/second/pallas_call | solution.py:171
  64.7 2.9 %last.1 = (bf16[2,192,384]{2,1,0:T(8,128)(2,1)S(1)}, bf16[2,192,384]{2,1,0:T(8,128)(2,1)S(1)}, bf16[2,2,192,384]{3,2,1,0:T(8,128)(2,1)S(1)}) custom-call(s32[2]{0:T(128)S(1)} %pad_add_fusion.scal, bf16[2,96,1536]{2,1,0:T(8,128)(2,1)S(1)} %collective-permute-done.16.refs_0_, bf16[4,96,1536]{2,1,0:T(8,128)(2,1)S(1)} %bitcast.39, ...), custom_call_target="tpu_custom_call" | custom-call | flops 1048576 | bytes 1048576 | tf_op jit(solution)/shard_map/last/pallas_call | solution.py:171
  67.6 0.6 collective-permute-start.18
  68.1 0.1 collective-permute-start.17
  68.2 0.9 collective-permute-start.19
  69.1 2.4 %collective-permute-done.17.att1 = bf16[2,2,192,384]{3,2,1,0:T(8,128)(2,1)S(1)} collective-permute-done((bf16[2,2,192,384]{3,2,1,0:T(8,128)(2,1)S(1)}, bf16[2,2,192,384]{3,2,1,0:T(8,128)(2,1)S(1)}, u32[]{:S(2)}, u32[]{:S(2)}) %collective-permute-start.17) | collective-permute-done | bytes 589856 | tf_op jit(solution)/shard_map/ppermute | solution.py:20
  71.4 1.4 %mix.2.refs_0_ = f32[2,192,1536]{2,1,0:T(8,128)S(1)} custom-call(bf16[384,1536]{1,0:T(8,128)(2,1)S(1)} %copy-done.1, bf16[384,1536]{1,0:T(8,128)(2,1)S(1)} %copy-done, bf16[384,1536]{1,0:T(8,128)(2,1)S(1)} %bitcast.43, bf16[2,192,384]{2,1,0:T(8,128)(2,1)S(1)} %get-tuple-element.117.att0, bf16[2,2,192,384]{3,2,1,0:T(8,128)(2,1)S(1)} %collective-permute-done.17.att1, ...), custom_call_target="tpu_custom_call" | custom-call | flops 905969664 | bytes 8388608 | tf_op jit(solution)/shard_map/mix/pallas_call | solution.py:198
  72.9 2.7 %mix.3 = (f32[2,192,1536]{2,1,0:T(8,128)S(1)}, bf16[384,768]{1,0:T(8,128)(2,1)S(1)}) custom-call(bf16[384,1536]{1,0:T(8,128)(2,1)S(1)} %copy-done.1, bf16[384,1536]{1,0:T(8,128)(2,1)S(1)} %copy-done, bf16[384,1536]{1,0:T(8,128)(2,1)S(1)} %bitcast.44, bf16[2,192,384]{2,1,0:T(8,128)(2,1)S(1)} %get-tuple-element.121.att0, ...), custom_call_target="tpu_custom_call" | custom-call | flops 905969664 | bytes 8388608 | tf_op jit(solution)/shard_map/mix/pallas_call | solution.py:198
  75.6 0.4 collective-permute-start.21
  76.0 0.1 collective-permute-start.22
  76.1 1.4 %collective-permute-done.19.refs_4_ = bf16[2,192,384]{2,1,0:T(8,128)(2,1)S(1)} collective-permute-done((bf16[2,192,384]{2,1,0:T(8,128)(2,1)S(1)}, bf16[2,192,384]{2,1,0:T(8,128)(2,1)S(1)}, u32[]{:S(2)}, u32[]{:S(2)}) %collective-permute-start.19) | collective-permute-done | bytes 294944 | tf_op jit(solution)/shard_map/ppermute | solution.py:20
  77.6 0.9 collective-permute-start.23
  78.4 0.7 collective-permute-done.20.refs_5_
  79.2 5.0 %middle.2 = (bf16[2,192,384]{2,1,0:T(8,128)(2,1)S(1)}, bf16[2,192,384]{2,1,0:T(8,128)(2,1)S(1)}, f32[192,384]{1,0:T(8,128)S(1)}) custom-call(s32[2]{0:T(128)S(1)} %pad_add_fusion.scal, f32[2,192,1536]{2,1,0:T(8,128)S(1)} %mix.2.refs_0_, f32[1,1536]{1,0:T(1,128)S(1)} %reshape.23.refs_1_, bf16[1536,768]{1,0:T(8,128)(2,1)S(1)} %copy-done.6, ...), custom_call_target="tpu_custom_call" | custom-call | flops 2717908992 | bytes 14680064 | tf_op jit(solution)/shard_map/middle/pallas_call | solution.py:247
  84.1 2.8 %collective-permute-done.23.refs_4_ = bf16[2,192,384]{2,1,0:T(8,128)(2,1)S(1)} collective-permute-done((bf16[2,192,384]{2,1,0:T(8,128)(2,1)S(1)}, bf16[2,192,384]{2,1,0:T(8,128)(2,1)S(1)}, u32[]{:S(2)}, u32[]{:S(2)}) %collective-permute-start.23) | collective-permute-done | bytes 294944 | tf_op jit(solution)/shard_map/ppermute | solution.py:20
  87.0 0.5 collective-permute-start.25
  87.5 1.1 %collective-permute-done.24 = bf16[2,192,384]{2,1,0:T(8,128)(2,1)S(1)} collective-permute-done((bf16[2,192,384]{2,1,0:T(8,128)(2,1)S(1)}, bf16[2,192,384]{2,1,0:T(8,128)(2,1)S(1)}, u32[]{:S(2)}, u32[]{:S(2)}) %collective-permute-start.24) | collective-permute-done | bytes 294944 | tf_op jit(solution)/shard_map/ppermute | solution.py:20
  88.6 0.1 convert_add_fusion.1
  88.7 0.9 collective-permute-start.26
  89.6 4.8 %middle.3 = (bf16[2,192,384]{2,1,0:T(8,128)(2,1)S(1)}, bf16[2,192,384]{2,1,0:T(8,128)(2,1)S(1)}, f32[192,384]{1,0:T(8,128)S(1)}) custom-call(s32[2]{0:T(128)S(1)} %pad_add_fusion.scal, f32[2,192,1536]{2,1,0:T(8,128)S(1)} %get-tuple-element.140.refs_0_, f32[1,1536]{1,0:T(1,128)S(1)} %reshape.23.refs_1_, bf16[1536,768]{1,0:T(8,128)(2,1)S(1)} %copy-done.6, ...), custom_call_target="tpu_custom_call" | custom-call | flops 2717908992 | bytes 14680064 | tf_op jit(solution)/shard_map/middle/pallas_call | solution.py:247
  94.4 0.2 collective-permute-done.26
  94.6 1.6 %collective-permute-done.27 = bf16[2,192,384]{2,1,0:T(8,128)(2,1)S(1)} collective-permute-done((bf16[2,192,384]{2,1,0:T(8,128)(2,1)S(1)}, bf16[2,192,384]{2,1,0:T(8,128)(2,1)S(1)}, u32[]{:S(2)}, u32[]{:S(2)}) %collective-permute-start.27) | collective-permute-done | bytes 294944 | tf_op jit(solution)/shard_map/ppermute | solution.py:20
  96.2 0.1 convert_add_fusion
  96.3 1.0 %collective-permute-start.28 = (bf16[192,384]{1,0:T(8,128)(2,1)S(1)}, bf16[192,384]{1,0:T(8,128)(2,1)S(1)}, u32[]{:S(2)}, u32[]{:S(2)}) collective-permute-start(bf16[192,384]{1,0:T(8,128)(2,1)S(1)} %fusion.9), channel_id=1, source_target_pairs={{0,2},{1,3},{2,0},{3,1},{4,6},{5,7},{6,4},{7,5},{8,10},{9,11},{10,... | collective-permute-start | bytes 442376 | tf_op jit(solution)/shard_map/ppermute | solution.py:20
  97.4 4.9 %collective-permute-done.28 = bf16[192,384]{1,0:T(8,128)(2,1)S(1)} collective-permute-done((bf16[192,384]{1,0:T(8,128)(2,1)S(1)}, bf16[192,384]{1,0:T(8,128)(2,1)S(1)}, u32[]{:S(2)}, u32[]{:S(2)}) %collective-permute-start.28) | collective-permute-done | bytes 147488 | tf_op jit(solution)/shard_map/ppermute | solution.py:20
  102.2 0.1 fusion.4
  102.3 0.9 pad_maximum_fusion
  (44 shorter events, 0.2 us)
Async XLA Ops:
  1.6 13.4 %collective-permute-start = (bf16[96,768]{1,0:T(8,128)(2,1)}, bf16[96,768]{1,0:T(8,128)(2,1)S(1)}, u32[]{:S(2)}, u32[]{:S(2)}) collective-permute-start(bf16[96,768]{1,0:T(8,128)(2,1)} %dynamic_slice.9), channel_id=1, source_target_pairs={{0,4},{1,5},{2,6},{3,7},{4,0},{5,1},{6,2},{7,3},{8,12},{9,13},{10,... | collective-permute-start | bytes 442376 | tf_op jit(solution)/shard_map/ppermute | solution.py:20
  4.6 14.2 %collective-permute-start.1 = (bf16[96,768]{1,0:T(8,128)(2,1)}, bf16[96,768]{1,0:T(8,128)(2,1)S(1)}, u32[]{:S(2)}, u32[]{:S(2)}) collective-permute-start(bf16[96,768]{1,0:T(8,128)(2,1)} %dynamic_slice.9), channel_id=1, source_target_pairs={{0,8},{1,9},{2,10},{3,11},{4,12},{5,13},{6,14},{7,15},{8,0},{9,1},... | collective-permute-start | bytes 442376 | tf_op jit(solution)/shard_map/ppermute | solution.py:20
  7.2 11.6 %collective-permute-start.2 = (bf16[96,768]{1,0:T(8,128)(2,1)}, bf16[96,768]{1,0:T(8,128)(2,1)}, u32[]{:S(2)}, u32[]{:S(2)}) collective-permute-start(bf16[96,768]{1,0:T(8,128)(2,1)} %dynamic_slice.9), channel_id=1, source_target_pairs={{0,12},{1,13},{2,14},{3,15},{4,8},{5,9},{6,10},{7,11},{8,4},{9,5},... | collective-permute-start | bytes 442376 | tf_op jit(solution)/shard_map/ppermute | solution.py:20
  9.1 27.7 %collective-permute-start.6 = (bf16[384,768]{1,0:T(8,128)(2,1)}, bf16[384,768]{1,0:T(8,128)(2,1)}, u32[]{:S(2)}, u32[]{:S(2)}) collective-permute-start(bf16[384,768]{1,0:T(8,128)(2,1)} %constant_dynamic-slice_fusion), channel_id=1, source_target_pairs={{0,2},{1,3},{2,0},{3,1},{4,6},{5,7},{6,4},{7,5},{8,10},{9,11},{10,... | collective-permute-start | bytes 1769480 | tf_op jit(solution)/shard_map/ppermute | solution.py:20
  10.8 2.8 %copy-start.8 = (bf16[1536,384]{1,0:T(8,128)(2,1)S(1)}, bf16[1536,384]{1,0:T(8,128)(2,1)}, u32[]{:S(2)}) copy-start(bf16[1536,384]{1,0:T(8,128)(2,1)} %param.14) | copy-start | bytes 3538948
  10.8 2.8 %copy-start.9 = (f32[1536]{0:T(1024)S(1)}, f32[1536]{0:T(1024)}, u32[]{:S(2)}) copy-start(f32[1536]{0:T(1024)} %param.12) | copy-start | bytes 18436
  13.6 24.6 %copy-start = (bf16[384,1536]{1,0:T(8,128)(2,1)S(1)}, bf16[384,1536]{1,0:T(8,128)(2,1)}, u32[]{:S(2)}) copy-start(bf16[384,1536]{1,0:T(8,128)(2,1)} %loc_ref.3) | copy-start | bytes 3538948
  13.6 24.5 %copy-start.5 = (f32[2]{0:T(128)S(1)}, f32[2]{0:T(128)}, u32[]{:S(2)}) copy-start(f32[2]{0:T(128)} %refs_5_.5) | copy-start | bytes 28
  13.9 24.3 %copy-start.1 = (bf16[384,1536]{1,0:T(8,128)(2,1)S(1)}, bf16[384,1536]{1,0:T(8,128)(2,1)}, u32[]{:S(2)}) copy-start(bf16[384,1536]{1,0:T(8,128)(2,1)} %x_ref.3) | copy-start | bytes 3538948
  19.7 13.6 %collective-permute-start.3 = (bf16[3,96,768]{2,1,0:T(8,128)(2,1)S(1)}, bf16[3,96,768]{2,1,0:T(8,128)(2,1)S(1)}, u32[]{:S(2)}, u32[]{:S(2)}) collective-permute-start(bf16[3,96,768]{2,1,0:T(8,128)(2,1)S(1)} %stack.16.refs_0_), channel_id=1, source_target_pairs={{0,2},{1,3},{2,0},{3,1},{4,6},{5,7},{6,4},{7,5},{8,10},{9,11},{10,... | collective-permute-start | bytes 1327112 | tf_op jit(solution)/shard_map/ppermute | solution.py:20
  21.3 15.5 %collective-permute-start.7 = (bf16[3,96,768]{2,1,0:T(8,128)(2,1)S(1)}, bf16[3,96,768]{2,1,0:T(8,128)(2,1)S(1)}, u32[]{:S(2)}, u32[]{:S(2)}) collective-permute-start(bf16[3,96,768]{2,1,0:T(8,128)(2,1)S(1)} %stack.16.refs_0_), channel_id=1, source_target_pairs={{0,16},{1,17},{2,18},{3,19},{4,20},{5,21},{6,22},{7,23},{8,24},{9,... | collective-permute-start | bytes 1327112 | tf_op jit(solution)/shard_map/ppermute | solution.py:20
  22.8 12.0 %collective-permute-start.4 = (bf16[1,96,1536]{2,1,0:T(8,128)(2,1)S(1)}, bf16[1,96,1536]{2,1,0:T(8,128)(2,1)S(1)}, u32[]{:S(2)}, u32[]{:S(2)}) collective-permute-start(bf16[1,96,1536]{2,1,0:T(8,128)(2,1)S(1)} %constant_dynamic-slice_fusion.1), channel_id=1, source_target_pairs={{0,12},{1,13},{2,14},{3,15},{4,8},{5,9},{6,10},{7,11},{8,4},{9,5},... | collective-permute-start | bytes 884744 | tf_op jit(solution)/shard_map/ppermute | solution.py:20
  25.1 11.7 %collective-permute-start.5 = (bf16[1,96,1536]{2,1,0:T(8,128)(2,1)S(1)}, bf16[1,96,1536]{2,1,0:T(8,128)(2,1)S(1)}, u32[]{:S(2)}, u32[]{:S(2)}) collective-permute-start(bf16[1,96,1536]{2,1,0:T(8,128)(2,1)S(1)} %constant_dynamic-slice_fusion.1), channel_id=1, source_target_pairs={{0,4},{1,5},{2,6},{3,7},{4,0},{5,1},{6,2},{7,3},{8,12},{9,13},{10,... | collective-permute-start | bytes 884744 | tf_op jit(solution)/shard_map/ppermute | solution.py:20
  33.3 11.8 %collective-permute-start.8 = (bf16[3,96,768]{2,1,0:T(8,128)(2,1)S(1)}, bf16[3,96,768]{2,1,0:T(8,128)(2,1)S(1)}, u32[]{:S(2)}, u32[]{:S(2)}) collective-permute-start(bf16[3,96,768]{2,1,0:T(8,128)(2,1)S(1)} %collective-permute-done.3.refs_1_), channel_id=1, source_target_pairs={{0,16},{1,17},{2,18},{3,19},{4,20},{5,21},{6,22},{7,23},{8,24},{9,... | collective-permute-start | bytes 1327112 | tf_op jit(solution)/shard_map/ppermute | solution.py:20
  36.8 7.8 %collective-permute-start.9 = (bf16[1,96,1536]{2,1,0:T(8,128)(2,1)S(1)}, bf16[1,96,1536]{2,1,0:T(8,128)(2,1)S(1)}, u32[]{:S(2)}, u32[]{:S(2)}) collective-permute-start(bf16[1,96,1536]{2,1,0:T(8,128)(2,1)S(1)} %collective-permute-done.4), channel_id=1, source_target_pairs={{0,4},{1,5},{2,6},{3,7},{4,0},{5,1},{6,2},{7,3},{8,12},{9,13},{10,... | collective-permute-start | bytes 884744 | tf_op jit(solution)/shard_map/ppermute | solution.py:20
  37.5 7.6 %collective-permute-start.10 = (bf16[1,96,1536]{2,1,0:T(8,128)(2,1)S(1)}, bf16[1,96,1536]{2,1,0:T(8,128)(2,1)S(1)}, u32[]{:S(2)}, u32[]{:S(2)}) collective-permute-start(bf16[1,96,1536]{2,1,0:T(8,128)(2,1)S(1)} %collective-permute-done.5), channel_id=1, source_target_pairs={{0,2},{1,3},{2,0},{3,1},{4,6},{5,7},{6,4},{7,5},{8,10},{9,11},{10,... | collective-permute-start | bytes 884744 | tf_op jit(solution)/shard_map/ppermute | solution.py:20
  38.1 1.1 %copy-start.3 = (bf16[1536,256]{1,0:T(8,128)(2,1)S(1)}, bf16[1536,256]{1,0:T(8,128)(2,1)}, u32[]{:S(2)}) copy-start(bf16[1536,256]{1,0:T(8,128)(2,1)} %get-tuple-element.82.refs_6_.refs_8_) | copy-start | bytes 2359300
  45.3 3.8 %copy-start.4 = (bf16[1536,256]{1,0:T(8,128)(2,1)S(1)}, bf16[1536,256]{1,0:T(8,128)(2,1)}, u32[]{:S(2)}) copy-start(bf16[1536,256]{1,0:T(8,128)(2,1)} %get-tuple-element.82.refs_6_.refs_8_) | copy-start | bytes 2359300
  45.3 3.8 %collective-permute-start.11 = (bf16[4,3,96,768]{3,2,1,0:T(8,128)(2,1)S(1)}, bf16[4,3,96,768]{3,2,1,0:T(8,128)(2,1)S(1)}, u32[]{:S(2)}, u32[]{:S(2)}) collective-permute-start(bf16[4,3,96,768]{3,2,1,0:T(8,128)(2,1)S(1)} %stack.17.refs_2_.refs_3_), channel_id=1, source_target_pairs={{0,1},{1,0},{2,3},{3,2},{4,5},{5,4},{6,7},{7,6},{8,9},{9,8},{10,11... | collective-permute-start | bytes 5308424 | tf_op jit(solution)/shard_map/ppermute | solution.py:20
  45.4 6.5 %collective-permute-start.12 = (bf16[4,96,1536]{2,1,0:T(8,128)(2,1)S(1)}, bf16[4,96,1536]{2,1,0:T(8,128)(2,1)S(1)}, u32[]{:S(2)}, u32[]{:S(2)}) collective-permute-start(bf16[4,96,1536]{2,1,0:T(8,128)(2,1)S(1)} %stack.18.refs_0_), channel_id=1, source_target_pairs={{0,1},{1,0},{2,3},{3,2},{4,5},{5,4},{6,7},{7,6},{8,9},{9,8},{10,11... | collective-permute-start | bytes 3538952 | tf_op jit(solution)/shard_map/ppermute | solution.py:20
  46.0 15.5 %collective-permute-start.13 = (bf16[384,768]{1,0:T(8,128)(2,1)}, bf16[384,768]{1,0:T(8,128)(2,1)S(1)}, u32[]{:S(2)}, u32[]{:S(2)}) collective-permute-start(bf16[384,768]{1,0:T(8,128)(2,1)} %collective-permute-done.6.refs_0_), channel_id=1, source_target_pairs={{0,16},{1,17},{2,18},{3,19},{4,20},{5,21},{6,22},{7,23},{8,24},{9,... | collective-permute-start | bytes 1769480 | tf_op jit(solution)/shard_map/ppermute | solution.py:20
  46.5 12.7 %collective-permute-start.15 = (bf16[1,96,1536]{2,1,0:T(8,128)(2,1)S(1)}, bf16[1,96,1536]{2,1,0:T(8,128)(2,1)S(1)}, u32[]{:S(2)}, u32[]{:S(2)}) collective-permute-start(bf16[1,96,1536]{2,1,0:T(8,128)(2,1)S(1)} %collective-permute-done.4), channel_id=1, source_target_pairs={{0,2},{1,3},{2,0},{3,1},{4,6},{5,7},{6,4},{7,5},{8,10},{9,11},{10,... | collective-permute-start | bytes 884744 | tf_op jit(solution)/shard_map/ppermute | solution.py:20
  47.4 14.2 %collective-permute-start.14 = (bf16[1,96,1536]{2,1,0:T(8,128)(2,1)S(1)}, bf16[1,96,1536]{2,1,0:T(8,128)(2,1)S(1)}, u32[]{:S(2)}, u32[]{:S(2)}) collective-permute-start(bf16[1,96,1536]{2,1,0:T(8,128)(2,1)S(1)} %collective-permute-done.9), channel_id=1, source_target_pairs={{0,2},{1,3},{2,0},{3,1},{4,6},{5,7},{6,4},{7,5},{8,10},{9,11},{10,... | collective-permute-start | bytes 884744 | tf_op jit(solution)/shard_map/ppermute | solution.py:20
  61.6 3.1 %collective-permute-start.16 = (bf16[2,96,1536]{2,1,0:T(8,128)(2,1)S(1)}, bf16[2,96,1536]{2,1,0:T(8,128)(2,1)S(1)}, u32[]{:S(2)}, u32[]{:S(2)}) collective-permute-start(bf16[2,96,1536]{2,1,0:T(8,128)(2,1)S(1)} %stack.19.refs_0_), channel_id=1, source_target_pairs={{0,1},{1,0},{2,3},{3,2},{4,5},{5,4},{6,7},{7,6},{8,9},{9,8},{10,11... | collective-permute-start | bytes 1769480 | tf_op jit(solution)/shard_map/ppermute | solution.py:20
  64.6 2.9 %copy-start.2 = (bf16[384,1536]{1,0:T(8,128)(2,1)S(1)}, bf16[384,1536]{1,0:T(8,128)(2,1)}, u32[]{:S(2)}) copy-start(bf16[384,1536]{1,0:T(8,128)(2,1)} %wo0.1) | copy-start | bytes 3538948
  67.6 3.9 %collective-permute-start.18 = (bf16[384,1536]{1,0:T(8,128)(2,1)S(1)}, bf16[384,1536]{1,0:T(8,128)(2,1)S(1)}, u32[]{:S(2)}, u32[]{:S(2)}) collective-permute-start(bf16[384,1536]{1,0:T(8,128)(2,1)S(1)} %copy-done.2), channel_id=1, source_target_pairs={{0,1},{1,0},{2,3},{3,2},{4,5},{5,4},{6,7},{7,6},{8,9},{9,8},{10,11... | collective-permute-start | bytes 3538952 | tf_op jit(solution)/shard_map/ppermute | solution.py:20
  68.1 3.3 %collective-permute-start.17 = (bf16[2,2,192,384]{3,2,1,0:T(8,128)(2,1)S(1)}, bf16[2,2,192,384]{3,2,1,0:T(8,128)(2,1)S(1)}, u32[]{:S(2)}, u32[]{:S(2)}) collective-permute-start(bf16[2,2,192,384]{3,2,1,0:T(8,128)(2,1)S(1)} %get-tuple-element.119), channel_id=1, source_target_pairs={{0,1},{1,0},{2,3},{3,2},{4,5},{5,4},{6,7},{7,6},{8,9},{9,8},{10,11... | collective-permute-start | bytes 1769480 | tf_op jit(solution)/shard_map/ppermute | solution.py:20
  68.2 9.4 %collective-permute-start.19 = (bf16[2,192,384]{2,1,0:T(8,128)(2,1)S(1)}, bf16[2,192,384]{2,1,0:T(8,128)(2,1)S(1)}, u32[]{:S(2)}, u32[]{:S(2)}) collective-permute-start(bf16[2,192,384]{2,1,0:T(8,128)(2,1)S(1)} %get-tuple-element.117.att0), channel_id=1, source_target_pairs={{0,2},{1,3},{2,0},{3,1},{4,6},{5,7},{6,4},{7,5},{8,10},{9,11},{10,... | collective-permute-start | bytes 884744 | tf_op jit(solution)/shard_map/ppermute | solution.py:20
  72.8 5.6 %copy-start.10 = (f32[1536]{0:T(1024)S(1)}, f32[1536]{0:T(1024)}, u32[]{:S(2)}) copy-start(f32[1536]{0:T(1024)} %param.17) | copy-start | bytes 18436
  72.9 6.3 %copy-start.6 = (bf16[1536,768]{1,0:T(8,128)(2,1)S(1)}, bf16[1536,768]{1,0:T(8,128)(2,1)}, u32[]{:S(2)}) copy-start(bf16[1536,768]{1,0:T(8,128)(2,1)} %refs_2_.3) | copy-start | bytes 7077892
  72.9 6.3 %copy-start.7 = (bf16[768,1536]{1,0:T(8,128)(2,1)S(1)}, bf16[768,1536]{1,0:T(8,128)(2,1)}, u32[]{:S(2)}) copy-start(bf16[768,1536]{1,0:T(8,128)(2,1)} %refs_3_.5) | copy-start | bytes 7077892
  75.6 3.6 %collective-permute-start.21 = (bf16[384,768]{1,0:T(8,128)(2,1)}, bf16[384,768]{1,0:T(8,128)(2,1)S(1)}, u32[]{:S(2)}, u32[]{:S(2)}) collective-permute-start(bf16[384,768]{1,0:T(8,128)(2,1)} %collective-permute-done.6.refs_0_), channel_id=1, source_target_pairs={{0,1},{1,0},{2,3},{3,2},{4,5},{5,4},{6,7},{7,6},{8,9},{9,8},{10,11... | collective-permute-start | bytes 1769480 | tf_op jit(solution)/shard_map/ppermute | solution.py:20
  76.0 3.1 %collective-permute-start.22 = (bf16[384,768]{1,0:T(8,128)(2,1)S(1)}, bf16[384,768]{1,0:T(8,128)(2,1)S(1)}, u32[]{:S(2)}, u32[]{:S(2)}) collective-permute-start(bf16[384,768]{1,0:T(8,128)(2,1)S(1)} %collective-permute-done.13.refs_8_), channel_id=1, source_target_pairs={{0,1},{1,0},{2,3},{3,2},{4,5},{5,4},{6,7},{7,6},{8,9},{9,8},{10,11... | collective-permute-start | bytes 1769480 | tf_op jit(solution)/shard_map/ppermute | solution.py:20
  77.6 1.6 %collective-permute-start.20 = (bf16[2,192,384]{2,1,0:T(8,128)(2,1)S(1)}, bf16[2,192,384]{2,1,0:T(8,128)(2,1)S(1)}, u32[]{:S(2)}, u32[]{:S(2)}) collective-permute-start(bf16[2,192,384]{2,1,0:T(8,128)(2,1)S(1)} %collective-permute-done.19.refs_4_), channel_id=1, source_target_pairs={{0,1},{1,0},{2,3},{3,2},{4,5},{5,4},{6,7},{7,6},{8,9},{9,8},{10,11... | collective-permute-start | bytes 884744 | tf_op jit(solution)/shard_map/ppermute | solution.py:20
  77.6 9.4 %collective-permute-start.23 = (bf16[2,192,384]{2,1,0:T(8,128)(2,1)S(1)}, bf16[2,192,384]{2,1,0:T(8,128)(2,1)S(1)}, u32[]{:S(2)}, u32[]{:S(2)}) collective-permute-start(bf16[2,192,384]{2,1,0:T(8,128)(2,1)S(1)} %get-tuple-element.121.att0), channel_id=1, source_target_pairs={{0,2},{1,3},{2,0},{3,1},{4,6},{5,7},{6,4},{7,5},{8,10},{9,11},{10,... | collective-permute-start | bytes 884744 | tf_op jit(solution)/shard_map/ppermute | solution.py:20
  87.0 1.6 %collective-permute-start.24 = (bf16[2,192,384]{2,1,0:T(8,128)(2,1)S(1)}, bf16[2,192,384]{2,1,0:T(8,128)(2,1)S(1)}, u32[]{:S(2)}, u32[]{:S(2)}) collective-permute-start(bf16[2,192,384]{2,1,0:T(8,128)(2,1)S(1)} %get-tuple-element.138), channel_id=1, source_target_pairs={{0,1},{1,0},{2,3},{3,2},{4,5},{5,4},{6,7},{7,6},{8,9},{9,8},{10,11... | collective-permute-start | bytes 884744 | tf_op jit(solution)/shard_map/ppermute | solution.py:20
  87.0 2.6 %collective-permute-start.25 = (bf16[2,192,384]{2,1,0:T(8,128)(2,1)S(1)}, bf16[2,192,384]{2,1,0:T(8,128)(2,1)S(1)}, u32[]{:S(2)}, u32[]{:S(2)}) collective-permute-start(bf16[2,192,384]{2,1,0:T(8,128)(2,1)S(1)} %collective-permute-done.23.refs_4_), channel_id=1, source_target_pairs={{0,1},{1,0},{2,3},{3,2},{4,5},{5,4},{6,7},{7,6},{8,9},{9,8},{10,11... | collective-permute-start | bytes 884744 | tf_op jit(solution)/shard_map/ppermute | solution.py:20
  88.7 6.0 %collective-permute-start.26 = (bf16[192,384]{1,0:T(8,128)(2,1)S(1)}, bf16[192,384]{1,0:T(8,128)(2,1)S(1)}, u32[]{:S(2)}, u32[]{:S(2)}) collective-permute-start(bf16[192,384]{1,0:T(8,128)(2,1)S(1)} %fusion.8), channel_id=1, source_target_pairs={{0,2},{1,3},{2,0},{3,1},{4,6},{5,7},{6,4},{7,5},{8,10},{9,11},{10,... | collective-permute-start | bytes 442376 | tf_op jit(solution)/shard_map/ppermute | solution.py:20
  94.6 1.6 %collective-permute-start.27 = (bf16[2,192,384]{2,1,0:T(8,128)(2,1)S(1)}, bf16[2,192,384]{2,1,0:T(8,128)(2,1)S(1)}, u32[]{:S(2)}, u32[]{:S(2)}) collective-permute-start(bf16[2,192,384]{2,1,0:T(8,128)(2,1)S(1)} %get-tuple-element.148), channel_id=1, source_target_pairs={{0,1},{1,0},{2,3},{3,2},{4,5},{5,4},{6,7},{7,6},{8,9},{9,8},{10,11... | collective-permute-start | bytes 884744 | tf_op jit(solution)/shard_map/ppermute | solution.py:20
  96.3 6.0 %collective-permute-start.28 = (bf16[192,384]{1,0:T(8,128)(2,1)S(1)}, bf16[192,384]{1,0:T(8,128)(2,1)S(1)}, u32[]{:S(2)}, u32[]{:S(2)}) collective-permute-start(bf16[192,384]{1,0:T(8,128)(2,1)S(1)} %fusion.9), channel_id=1, source_target_pairs={{0,2},{1,3},{2,0},{3,1},{4,6},{5,7},{6,4},{7,5},{8,10},{9,11},{10,... | collective-permute-start | bytes 442376 | tf_op jit(solution)/shard_map/ppermute | solution.py:20
